TPU v7x, 256 devices: a whole 4x4x8 slice. The times are simulated.
256 devices in a mesh: dp: 32 (over x, y, core), seq: 8 (over z).
Axes of the slice: x: 4, y: 4, z: 8, core: 2. Of those that a mesh axis runs over, the one named last changes fastest.
Arguments:
- queries: bfloat16 [32768, 8192], P(('dp', 'seq')), may hold values from -600 to 600
- output_gradient: bfloat16 [32768, 8192], P(('dp', 'seq')), may hold values from -6 to 6
- tiles: bfloat16 [512, 32, 7680], P('dp', None, 'seq'), may hold values from -6 to 6
- frozen_key_weight: bfloat16 [7680, 1024], P('seq'), may hold values from -0.0625 to 0.0625
- frozen_value_weight: bfloat16 [7680, 1024], P('seq'), may hold values from -0.0625 to 0.0625
- key_norm_gain: float32 [128], replicated, may hold values from 0.1 to 1.9
- adapter_down_weight: bfloat16 [7680, 16], P('seq'), may hold values from -0.0625 to 0.0625
- adapter_up_weight: bfloat16 [16, 1024], P(None, 'seq'), may hold values from -1.5 to 1.5
- gate: float32 [1], replicated, may hold values from 0.3 to 1.5
- document_lengths: int32 [32, 4], P('dp'), may hold values from 1 to 512, 1024 in all within a row
- image_reader_group: int32 [512], P('dp'), may hold values from 0 to 31, as said below
- image_document: int32 [512], P('dp'), may hold values from 0 to 3, as said below
Outputs:
- gated: bfloat16 [32768, 8192], P(('dp', 'seq'))
- query_grad: bfloat16 [32768, 8192], P(('dp', 'seq'))
- down_grad: float32 [7680, 16], P('seq')
- up_weight_gradient: float32 [16, 1024], P(None, 'seq')
Inputs may be any that keep to these rules, and one draw needn't show every extreme that they name: `image_reader_group`: the 16 images of one encoder shard go to 16 different groups; every group reads at least 4 images. `image_document`: every document of every group has at least one image.
All inputs are finite; a program needn't handle non-finite values.
Results may differ from a plain program's by a relative error of at most 0.029.
The roundings to bfloat16 on the way count: a program that leaves them out, or rounds other values in their place, can miss the bound.
Values may be sent and summed in bfloat16 or wider, within the bound.
A program may use at most 192 MiB of HBM per device.

v0:
```python
import jax
import jax.numpy as jnp
from jax import lax
from jax.sharding import PartitionSpec as P

EPS = 1e-05
ADAPTER_SCALE = 2.0


def attend(queries, attn_grad, key_rows, value_matrix_rows, tok_doc, key_doc, gate_value):
    num_rows = queries.shape[0]
    kv_heads, key_count, head_extent = key_rows.shape
    group_size = queries.shape[1] // (kv_heads * head_extent)
    score_scale = head_extent ** (-0.5)
    block_rows = min(512, num_rows)
    query_four = queries.reshape(num_rows, kv_heads, group_size, head_extent)
    grad_four = attn_grad.reshape(num_rows, kv_heads, group_size, head_extent)
    gated_parts = []
    qgrad_parts = []
    value_sums = [jnp.zeros((key_count, head_extent), jnp.float32)]
    for first_row in range(0, num_rows, block_rows):
        allowed = tok_doc[first_row : first_row + block_rows, None] == key_doc[None, :]
        query_block = query_four[first_row : first_row + block_rows, 0]
        grad_block = grad_four[first_row : first_row + block_rows, 0]
        scores = (
            jnp.einsum("ngd,md->gnm", query_block, key_rows[0], preferred_element_type=jnp.float32)
            * score_scale
        )
        scores = jnp.where(allowed[None], scores, -1e30)
        row_max = jnp.max(scores, axis=-1, keepdims=True)
        weights = jnp.exp(scores - row_max)
        prob_f32 = weights / jnp.sum(weights, axis=-1, keepdims=True)
        prob_bf16 = prob_f32.astype(jnp.bfloat16)
        attended = jnp.einsum(
            "gnm,md->ngd", prob_bf16, value_matrix_rows[0], preferred_element_type=jnp.float32
        )
        gated_heads = [(gate_value * attended).astype(jnp.bfloat16)]
        row_delta = jnp.sum(grad_block.astype(jnp.float32) * attended, axis=-1)
        prob_grad = jnp.einsum(
            "ngd,md->gnm", grad_block, value_matrix_rows[0], preferred_element_type=jnp.float32
        )
        score_grad = (prob_f32 * (prob_grad - row_delta.T[:, :, None])).astype(jnp.bfloat16)
        query_grad = (
            jnp.einsum("gnm,md->ngd", score_grad, key_rows[0], preferred_element_type=jnp.float32)
            * score_scale
        )
        qgrad_heads = [query_grad.astype(jnp.bfloat16)]
        value_sums[0] = value_sums[0] + jnp.einsum(
            "gnm,ngd->md", prob_bf16, grad_block, preferred_element_type=jnp.float32
        )
        gated_parts.append(jnp.stack(gated_heads, axis=1))
        qgrad_parts.append(jnp.stack(qgrad_heads, axis=1))
    gated = jnp.concatenate(gated_parts, axis=0).reshape(num_rows, -1)
    query_grad = jnp.concatenate(qgrad_parts, axis=0).reshape(num_rows, -1)
    return (gated, query_grad, jnp.stack(value_sums, axis=0))


def token_docs(positions, lengths):
    doc_ends = jnp.cumsum(lengths)
    return 1 + jnp.sum((positions[:, None] >= doc_ends[None, :-1]).astype(jnp.int32), axis=1)


def per_device(
    queries,
    output_gradient,
    tiles,
    frozen_key_weight,
    frozen_value_weight,
    key_norm_gain,
    adapter_down_weight,
    adapter_up_weight,
    gate,
    document_lengths,
    image_reader_group,
    image_document,
):
    seq_count = lax.axis_size("seq")
    group_count = lax.axis_size("dp")
    img_dev, rows_img, width_dev = tiles.shape
    head_extent = key_norm_gain.shape[0]
    kv_total = frozen_key_weight.shape[1] // head_extent
    kv_dev = kv_total // seq_count
    flattened_rows = tiles.reshape(img_dev * rows_img, width_dev)
    key_part = jnp.dot(
        flattened_rows, frozen_key_weight, preferred_element_type=jnp.float32
    ).reshape(-1, lax.axis_size("seq") * kv_dev, head_extent)
    value_part = jnp.dot(
        flattened_rows, frozen_value_weight, preferred_element_type=jnp.float32
    ).reshape(-1, lax.axis_size("seq") * kv_dev, head_extent)
    projected_rows = lax.psum_scatter(
        jnp.concatenate([key_part, value_part], axis=-1).transpose(1, 0, 2),
        "seq",
        scatter_dimension=0,
        tiled=True,
    )
    reduced_piece = jnp.dot(flattened_rows, adapter_down_weight, preferred_element_type=jnp.float32)
    reduced_rows = lax.psum(reduced_piece.astype(jnp.bfloat16), "seq")
    key_raw = projected_rows[..., :head_extent]
    mean_square = jnp.mean(key_raw * key_raw, axis=-1, keepdims=True)
    key_rows = (key_raw * lax.rsqrt(mean_square + EPS) * key_norm_gain).astype(jnp.bfloat16)
    reduced_up_output = (
        jnp.dot(reduced_rows, adapter_up_weight, preferred_element_type=jnp.float32)
        .reshape(-1, kv_dev, head_extent)
        .transpose(1, 0, 2)
    )
    value_matrix_rows = (
        projected_rows[..., head_extent:] + ADAPTER_SCALE * reduced_up_output
    ).astype(jnp.bfloat16)
    key_value = jnp.concatenate([key_rows, value_matrix_rows], axis=-1).reshape(
        kv_dev, img_dev, rows_img, 2 * head_extent
    )
    groups = jnp.arange(group_count, dtype=jnp.int32)
    picked = (image_reader_group[None, :] == groups[:, None]).astype(jnp.bfloat16)
    outgoing = jnp.einsum(
        "gt,htrc->ghrc", picked, key_value, preferred_element_type=jnp.float32
    ).astype(jnp.bfloat16)
    doc_marks = (image_document + 1).astype(jnp.bfloat16)[:, None]
    doc_tags = jnp.dot(picked, doc_marks, preferred_element_type=jnp.float32).astype(jnp.bfloat16)
    received, received_tags = (
        lax.all_to_all(outgoing, "dp", split_axis=0, concat_axis=0, tiled=True),
        lax.all_to_all(doc_tags, "dp", split_axis=0, concat_axis=0, tiled=True),
    )
    key_doc = jnp.repeat(received_tags[:, 0], rows_img).astype(jnp.int32)
    gate_value = jnp.tanh(gate[0])
    attn_grad = (gate_value * output_gradient.astype(jnp.float32)).astype(jnp.bfloat16)
    lengths = document_lengths[0]
    head_queries, head_grads = (
        lax.all_to_all(queries, "seq", split_axis=1, concat_axis=0, tiled=True),
        lax.all_to_all(attn_grad, "seq", split_axis=1, concat_axis=0, tiled=True),
    )
    head_rows = received.transpose(1, 0, 2, 3).reshape(
        kv_dev, group_count * rows_img, 2 * head_extent
    )
    positions = jnp.arange(head_queries.shape[0], dtype=jnp.int32)
    head_gated, head_qgrad, value_part = attend(
        head_queries,
        head_grads,
        head_rows[..., :head_extent],
        head_rows[..., head_extent:],
        token_docs(positions, lengths),
        key_doc,
        gate_value,
    )
    gated, query_grad = (
        lax.all_to_all(head_gated, "seq", split_axis=0, concat_axis=1, tiled=True),
        lax.all_to_all(head_qgrad, "seq", split_axis=0, concat_axis=1, tiled=True),
    )
    value_own = value_part.reshape(kv_dev, group_count, rows_img, head_extent)
    value_send = value_own.astype(jnp.bfloat16).transpose(1, 0, 2, 3)
    returned = lax.all_to_all(value_send, "dp", split_axis=0, concat_axis=0, tiled=True)
    value_images = jnp.einsum("gt,ghrd->htrd", picked, returned, preferred_element_type=jnp.float32)
    value_gradient = (
        value_images.transpose(1, 2, 0, 3)
        .reshape(img_dev * rows_img, kv_dev * head_extent)
        .astype(jnp.bfloat16)
    )
    up_weight_piece = ADAPTER_SCALE * jnp.dot(
        reduced_rows.T, value_gradient, preferred_element_type=jnp.float32
    )
    reduced_gradient_piece = ADAPTER_SCALE * jnp.dot(
        value_gradient, adapter_up_weight.T, preferred_element_type=jnp.float32
    )
    reduced_gradient = lax.psum(reduced_gradient_piece.astype(jnp.bfloat16), "seq")
    down_part = jnp.dot(flattened_rows.T, reduced_gradient, preferred_element_type=jnp.float32)
    down_grad, up_weight_gradient = (
        lax.psum(down_part.astype(jnp.bfloat16), "dp").astype(jnp.float32),
        lax.psum(up_weight_piece.astype(jnp.bfloat16), "dp").astype(jnp.float32),
    )
    return (gated, query_grad, down_grad, up_weight_gradient)


def solution(mesh):
    placed = (
        P(("dp", "seq"), None),
        P(("dp", "seq"), None),
        P("dp", None, "seq"),
        P("seq", None),
        P("seq", None),
        P(),
        P("seq", None),
        P(None, "seq"),
        P(),
        P("dp", None),
        P("dp"),
        P("dp"),
    )
    return jax.shard_map(
        per_device,
        mesh=mesh,
        in_specs=placed,
        out_specs=(P(("dp", "seq"), None), P(("dp", "seq"), None), P("seq", None), P(None, "seq")),
        check_vma=False,
    )
```

profile of v0, /device:TPU:1, one launch (start us, length us, event | category | flops | bytes accessed | tf_op | source)
XLA Modules:
  0.0 580.9 jit_solution(18195207550017957001)
XLA Ops:
  7.2 1.5 copy-done
  8.7 2.7 fusion.25
  11.4 1.3 fusion.22
  12.7 2.4 maximum_bitcast_fusion
  15.1 0.6 copy-done.12
  15.8 0.2 fusion.39
  16.0 0.7 copy.135
  16.7 8.6 %all-to-all-start.1 = ((bf16[32,1,1]{2,1,0:T(2,128)(2,1)}), bf16[32,1,1]{2,1,0:T(2,128)(2,1)S(1)}, u32[]{:S(2)}, u32[]{:S(2)}) async-start(bf16[32,1,1]{2,1,0:T(2,128)(2,1)} %copy.135), calls=%async_computation.2 | async-start | bytes 32768 | tf_op jit(solution)/shard_map/all_to_all | solution.py:121
  25.3 3.2 copy.208
  28.5 3.7 all-to-all-done.1
  32.2 8.2 %all-to-all-start.2 = ((bf16[128,8,1024]{2,0,1:T(8,128)(2,1)}), bf16[128,8,1024]{2,0,1:T(8,128)(2,1)}, u32[]{:S(2)}, u32[]{:S(2)}) async-start(bf16[128,8,1024]{2,0,1:T(8,128)(2,1)} %bitcast.216), calls=%async_computation.3 | async-start | bytes 4194304 | tf_op jit(solution)/shard_map/all_to_all | solution.py:128
  41.0 3.3 multiply_convert_fusion
  44.4 4.1 copy.143
  48.5 65.8 %all-to-all-done.2 = bf16[128,8,1024]{2,0,1:T(8,128)(2,1)} async-done(((bf16[128,8,1024]{2,0,1:T(8,128)(2,1)}), bf16[128,8,1024]{2,0,1:T(8,128)(2,1)}, u32[]{:S(2)}, u32[]{:S(2)}) %all-to-all-start.2) | async-done | bytes 2097184 | tf_op jit(solution)/shard_map/all_to_all | solution.py:128
  114.3 4.4 all-to-all-start.4
  118.7 0.2 reduce-window.4
  118.9 0.4 convolution_convert_fusion.3
  119.3 64.5 %psum.28 = bf16[512,16]{0,1:T(8,128)(2,1)S(1)} all-reduce(bf16[512,16]{0,1:T(8,128)(2,1)S(1)} %convolution_convert_fusion.3), channel_id=1, replica_groups=mesh['dp'=32,'seq'=8] {'seq'}, use_global_device_ids=true, to_apply=%region_2.0 | all-reduce | flops 8192 | bytes 32768 | tf_op jit(solution)/shard_map/psum | solution.py:97
  183.9 0.7 convert_reduce_fusion
  184.7 1.5 broadcast_compare_fusion.1
  186.2 1.0 multiply_reduce_fusion
  187.2 1.0 multiply_convert_fusion.3
  188.2 1.2 fusion.33
  189.6 0.4 fusion.28
  190.0 1.1 copy.133
  191.1 10.8 %all-to-all-start = ((bf16[32,1,32,256]{3,2,1,0:T(8,128)(2,1)}), bf16[32,1,32,256]{3,2,1,0:T(8,128)(2,1)S(1)}, u32[]{:S(2)}, u32[]{:S(2)}) async-start(bf16[32,1,32,256]{3,2,1,0:T(8,128)(2,1)} %copy.133), calls=%async_computation.1 | async-start | bytes 1048576 | tf_op jit(solution)/shard_map/all_to_all | solution.py:120
  201.9 1.7 fusion.63
  203.6 0.3 copy.187
  203.9 0.3 copy.188
  204.2 2.7 fusion.62
  206.8 1.8 copy.144
  208.6 2.3 squeeze.31
  210.9 3.0 copy.149
  213.9 2.2 squeeze.32
  216.1 8.1 %fusion.40 = f32[1024,512,8]{1,0,2:T(8,128)} fusion(bf16[512,8,128]{2,1,0:T(8,128)(2,1)S(1)} %bitcast.220, bf16[1,1024,256]{2,1,0:T(8,128)(2,1)S(1)} %bitcast.221), kind=kOutput, calls=%fused_computation.69 | convolution fusion | flops 1073741824 | bytes 18087936 | tf_op jit(solution)/shard_map/ngd,md->gnm/dot_general | solution.py:26
  224.2 17.8 %fusion.65 = (f32[8,512]{1,0:T(8,128)S(1)}, f32[8,512,1024]{1,2,0:T(8,128)}) fusion(f32[1024,512,8]{1,0,2:T(8,128)} %fusion.40, pred[512,1024]{0,1:T(8,128)(4,1)} %get-tuple-element.23), kind=kOutput, calls=%fused_computation.107 | output fusion | flops 25166848 | bytes 34095104 | tf_op jit(solution)/shard_map/sub | solution.py:31
  241.9 7.0 %fusion.15 = bf16[8,512,1024]{1,2,0:T(8,128)(2,1)S(1)} fusion(f32[8,512,1024]{1,2,0:T(8,128)} %get-tuple-element.27, f32[8,512]{1,0:T(8,128)S(1)} %get-tuple-element.26), kind=kLoop, calls=%fused_computation.23 | loop fusion | flops 8388608 | bytes 25182208 | tf_op jit(solution)/shard_map/convert_element_type | solution.py:33
  249.0 3.1 convolution_bitcast_fusion
  252.1 2.3 fusion.19
  254.4 8.0 %fusion.42 = f32[1024,512,8]{1,0,2:T(8,128)} fusion(bf16[512,8,128]{2,1,0:T(8,128)(2,1)S(1)} %bitcast.219, bf16[1,1024,256]{2,1,0:T(8,128)(2,1)S(1)} %bitcast.223), kind=kOutput, calls=%fused_computation.71 | convolution fusion | flops 1073741824 | bytes 18087936 | tf_op jit(solution)/shard_map/ngd,md->gnm/dot_general | solution.py:26
  262.5 17.5 %fusion.66 = (f32[8,512]{1,0:T(8,128)S(1)}, f32[8,512,1024]{1,2,0:T(8,128)}) fusion(f32[1024,512,8]{1,0,2:T(8,128)} %fusion.42, pred[512,1024]{0,1:T(8,128)(4,1)S(1)} %get-tuple-element.22), kind=kOutput, calls=%fused_computation.108 | output fusion | flops 25166848 | bytes 34095104 | tf_op jit(solution)/shard_map/sub | solution.py:31
  280.0 7.0 %fusion.14 = bf16[8,512,1024]{1,2,0:T(8,128)(2,1)S(1)} fusion(f32[8,512,1024]{1,2,0:T(8,128)} %get-tuple-element.29, f32[8,512]{1,0:T(8,128)S(1)} %get-tuple-element.28), kind=kLoop, calls=%fused_computation.22 | loop fusion | flops 8388608 | bytes 25182208 | tf_op jit(solution)/shard_map/convert_element_type | solution.py:33
  287.0 3.3 fusion.30
  290.3 7.8 %all-to-all-start.6 = ((bf16[32,1,32,128]{3,2,1,0:T(8,128)(2,1)}), bf16[32,1,32,128]{3,2,1,0:T(8,128)(2,1)S(1)}, u32[]{:S(2)}, u32[]{:S(2)}) async-start(bf16[32,1,32,128]{3,2,1,0:T(8,128)(2,1)} %bitcast.51), calls=%async_computation.7 | async-start | bytes 524288 | tf_op jit(solution)/shard_map/all_to_all | solution.py:150
  298.2 4.8 fusion.21
  303.0 1.6 pad_maximum_fusion
  304.6 3.9 copy.141
  308.5 4.4 all-to-all-start.3
  312.9 10.2 %multiply_convert_fusion.1 = bf16[128,8,512]{2,0,1:T(8,128)(2,1)} fusion(bf16[512,8,128]{0,2,1:T(8,128)(2,1)S(1)} %copy-done.6, f32[8,512]{1,0:T(8,128)S(1)} %bitcast.241, f32[8,512,1024]{1,2,0:T(8,128)} %get-tuple-element.27, f32[8,512]{1,0:T(8,128)S(1)} %get-tuple-element.26, bf16[1,1024,256]{2,1,0:T(8,128)(2,1)S(1)} %bitcast.225), kind=kOutput, calls=%fused_computation.39 | convolution fusion | flops 2165309440 | bytes 19431424 | tf_op jit(solution)/shard_map/gnm,md->ngd/dot_general | solution.py:44
  323.1 10.3 %multiply_convert_fusion.2 = bf16[128,8,512]{2,0,1:T(8,128)(2,1)} fusion(bf16[512,8,128]{0,2,1:T(8,128)(2,1)S(1)} %copy-done.5, f32[8,512]{1,0:T(8,128)S(1)} %bitcast.242, f32[8,512,1024]{1,2,0:T(8,128)} %get-tuple-element.29, f32[8,512]{1,0:T(8,128)S(1)} %get-tuple-element.28, bf16[1,1024,256]{2,1,0:T(8,128)(2,1)S(1)} %bitcast.226), kind=kOutput, calls=%fused_computation.40 | convolution fusion | flops 2165309440 | bytes 19431424 | tf_op jit(solution)/shard_map/gnm,md->ngd/dot_general | solution.py:44
  333.4 2.9 pad_maximum_fusion.1
  336.2 4.0 copy.154
  340.3 21.0 %all-to-all-done.3 = bf16[8,128,1024]{2,1,0:T(8,128)(2,1)} async-done(((bf16[8,128,1024]{2,1,0:T(8,128)(2,1)}), bf16[8,128,1024]{2,1,0:T(8,128)(2,1)}, u32[]{:S(2)}, u32[]{:S(2)}) %all-to-all-start.3) | async-done | bytes 2097184 | tf_op jit(solution)/shard_map/all_to_all | solution.py:145
  361.2 4.8 all-to-all-start.5
  366.0 0.2 fusion.34
  366.4 63.3 %psum.29 = bf16[512,16]{0,1:T(8,128)(2,1)S(1)} all-reduce(bf16[512,16]{0,1:T(8,128)(2,1)S(1)} %fusion.36), channel_id=1, replica_groups=mesh['dp'=32,'seq'=8] {'seq'}, use_global_device_ids=true, to_apply=%region_11.12 | all-reduce | flops 8192 | bytes 32768 | tf_op jit(solution)/shard_map/psum | solution.py:163
  429.8 0.2 fusion.35
  430.1 126.4 %all-reduce = (bf16[960,16]{0,1:T(8,128)(2,1)S(1)}, bf16[16,128]{1,0:T(8,128)(2,1)S(1)}) all-reduce(bf16[960,16]{0,1:T(8,128)(2,1)S(1)} %fusion.35, bf16[16,128]{1,0:T(8,128)(2,1)S(1)} %fusion.37), channel_id=1, replica_groups=mesh['dp'=32,'seq'=8] {'dp'}, use_global_device_ids=true, to_apply=%region_12.13 | all-reduce | flops 17408 | bytes 69632 | tf_op jit(solution)/shard_map/psum | solution.py:166
  556.5 0.6 convert_element_type.163
  557.1 0.6 convert_element_type.161
  557.7 3.9 copy.142
  561.6 4.2 copy.161
  565.8 3.9 copy.155
  569.7 4.1 copy.162
  (55 shorter events, 0.9 us)
Async XLA Ops:
  7.2 1.6 copy-start
  7.2 179.0 %reduce-scatter.2.cloned.1.call-start = ((), (), s32[]{:S(2)}) async-start(), calls=%async_computation.8 | async-start | bytes 4718592 | tf_op jit(solution)/shard_map/reduce_scatter | solution.py:90
  8.7 2.7 copy-start.3
  8.7 2.7 copy-start.15
  15.1 0.7 copy-start.12
  15.1 0.7 copy-start.16
  16.7 15.5 %all-to-all-start.1 = ((bf16[32,1,1]{2,1,0:T(2,128)(2,1)}), bf16[32,1,1]{2,1,0:T(2,128)(2,1)S(1)}, u32[]{:S(2)}, u32[]{:S(2)}) async-start(bf16[32,1,1]{2,1,0:T(2,128)(2,1)} %copy.135), calls=%async_computation.2 | async-start | bytes 32768 | tf_op jit(solution)/shard_map/all_to_all | solution.py:121
  32.2 82.2 %all-to-all-start.2 = ((bf16[128,8,1024]{2,0,1:T(8,128)(2,1)}), bf16[128,8,1024]{2,0,1:T(8,128)(2,1)}, u32[]{:S(2)}, u32[]{:S(2)}) async-start(bf16[128,8,1024]{2,0,1:T(8,128)(2,1)} %bitcast.216), calls=%async_computation.3 | async-start | bytes 4194304 | tf_op jit(solution)/shard_map/all_to_all | solution.py:128
  44.4 74.3 %copy-start.17 = (s32[1,4]{1,0:T(1,128)S(1)}, s32[1,4]{1,0:T(1,128)}, u32[]{:S(2)}) copy-start(s32[1,4]{1,0:T(1,128)} %param.21) | copy-start | bytes 52
  44.4 74.5 %copy-start.9 = (bf16[960,16]{0,1:T(8,128)(2,1)S(1)}, bf16[960,16]{0,1:T(8,128)(2,1)}, u32[]{:S(2)}) copy-start(bf16[960,16]{0,1:T(8,128)(2,1)} %param.18) | copy-start | bytes 92164
  48.5 138.7 %copy-start.14 = (f32[128]{0:T(128)S(1)}, f32[128]{0:T(128)}, u32[]{:S(2)}) copy-start(f32[128]{0:T(128)} %param.17) | copy-start | bytes 1540
  48.5 139.7 %copy-start.10 = (bf16[16,128]{1,0:T(8,128)(2,1)S(1)}, bf16[16,128]{1,0:T(8,128)(2,1)}, u32[]{:S(2)}) copy-start(bf16[16,128]{1,0:T(8,128)(2,1)} %param.19) | copy-start | bytes 12292
  114.3 76.7 %all-to-all-start.4 = ((bf16[128,8,1024]{0,2,1:T(8,128)(2,1)}), bf16[128,8,1024]{0,2,1:T(8,128)(2,1)}, u32[]{:S(2)}, u32[]{:S(2)}) async-start(bf16[128,8,1024]{0,2,1:T(8,128)(2,1)} %bitcast.213), calls=%async_computation.5 | async-start | bytes 4194304 | tf_op jit(solution)/shard_map/all_to_all | solution.py:129
  191.1 25.0 %all-to-all-start = ((bf16[32,1,32,256]{3,2,1,0:T(8,128)(2,1)}), bf16[32,1,32,256]{3,2,1,0:T(8,128)(2,1)S(1)}, u32[]{:S(2)}, u32[]{:S(2)}) async-start(bf16[32,1,32,256]{3,2,1,0:T(8,128)(2,1)} %copy.133), calls=%async_computation.1 | async-start | bytes 1048576 | tf_op jit(solution)/shard_map/all_to_all | solution.py:120
  241.9 7.0 %copy-start.6 = (bf16[512,8,128]{0,2,1:T(8,128)(2,1)S(1)}, bf16[512,8,128]{0,2,1:T(8,128)(2,1)}, u32[]{:S(2)}) copy-start(bf16[512,8,128]{0,2,1:T(8,128)(2,1)} %squeeze.32) | copy-start | bytes 3145732
  280.0 7.0 %copy-start.5 = (bf16[512,8,128]{0,2,1:T(8,128)(2,1)S(1)}, bf16[512,8,128]{0,2,1:T(8,128)(2,1)}, u32[]{:S(2)}) copy-start(bf16[512,8,128]{0,2,1:T(8,128)(2,1)} %squeeze.31) | copy-start | bytes 3145732
  280.0 7.0 %copy-start.18 = (f32[1024,128]{1,0:T(8,128)S(1)}, f32[1024,128]{1,0:T(8,128)}, u32[]{:S(2)}) copy-start(f32[1024,128]{1,0:T(8,128)} %convolution_bitcast_fusion) | copy-start | bytes 1572868
  287.0 3.3 copy-start.2
  290.3 18.2 %all-to-all-start.6 = ((bf16[32,1,32,128]{3,2,1,0:T(8,128)(2,1)}), bf16[32,1,32,128]{3,2,1,0:T(8,128)(2,1)S(1)}, u32[]{:S(2)}, u32[]{:S(2)}) async-start(bf16[32,1,32,128]{3,2,1,0:T(8,128)(2,1)} %bitcast.51), calls=%async_computation.7 | async-start | bytes 524288 | tf_op jit(solution)/shard_map/all_to_all | solution.py:150
  298.1 4.8 copy-start.7
  308.5 52.7 %all-to-all-start.3 = ((bf16[8,128,1024]{2,1,0:T(8,128)(2,1)}), bf16[8,128,1024]{2,1,0:T(8,128)(2,1)}, u32[]{:S(2)}, u32[]{:S(2)}) async-start(bf16[8,128,1024]{2,1,0:T(8,128)(2,1)} %bitcast.215), calls=%async_computation.4 | async-start | bytes 4194304 | tf_op jit(solution)/shard_map/all_to_all | solution.py:145
  323.1 10.3 %copy-start.8 = (bf16[128,8,512]{2,0,1:T(8,128)(2,1)S(1)}, bf16[128,8,512]{2,0,1:T(8,128)(2,1)}, u32[]{:S(2)}) copy-start(bf16[128,8,512]{2,0,1:T(8,128)(2,1)} %multiply_convert_fusion.1) | copy-start | bytes 3145732
  336.2 29.8 %copy-start.13 = (s32[16]{0:T(128)S(1)}, s32[16]{0:T(128)}, u32[]{:S(2)}) copy-start(s32[16]{0:T(128)} %param.22) | copy-start | bytes 196
  336.2 30.1 %copy-start.11 = (bf16[16,128]{1,0:T(8,128)(2,1)S(1)}, bf16[16,128]{1,0:T(8,128)(2,1)}, u32[]{:S(2)}) copy-start(bf16[16,128]{1,0:T(8,128)(2,1)} %param.19) | copy-start | bytes 12292
  336.2 93.6 %copy-start.4 = (bf16[16,32,960]{2,1,0:T(8,128)(2,1)S(1)}, bf16[16,32,960]{2,1,0:T(8,128)(2,1)}, u32[]{:S(2)}) copy-start(bf16[16,32,960]{2,1,0:T(8,128)(2,1)} %param.14) | copy-start | bytes 2949124
  361.2 204.6 %all-to-all-start.5 = ((bf16[8,128,1024]{2,1,0:T(8,128)(2,1)}), bf16[8,128,1024]{2,1,0:T(8,128)(2,1)}, u32[]{:S(2)}, u32[]{:S(2)}) async-start(bf16[8,128,1024]{2,1,0:T(8,128)(2,1)} %bitcast.214), calls=%async_computation.6 | async-start | bytes 4194304 | tf_op jit(solution)/shard_map/all_to_all | solution.py:146
  561.6 12.2 %copy-start.1 = (bf16[960,1024]{1,0:T(8,128)(2,1)S(1)}, bf16[960,1024]{1,0:T(8,128)(2,1)}, u32[]{:S(2)}) copy-start(bf16[960,1024]{1,0:T(8,128)(2,1)} %param.15) | copy-start | bytes 5898244
Sparse Core Ops, SparseCore 0:
  15.3 104.0 reduce-scatter.1
where the time goes:
time: 591 us; the launch traced here: 581 us
  blocking collectives  254 us (43%)
  waiting for transfers between devices  90.5 us (15%)
  other arithmetic  65.1 us (11%)
  matrix products  57 us (10%)
  local copies, waits for them, and re-layouts  49.8 us (8%)
  starting transfers between devices  49 us (8%)
  between operations  15.3 us (3%)
    psum x1, blocking collectives, per_device(): lax.psum(down_part.astype(jnp.bfloat16), 'dp').astype(jnp.float32)  126 us
    all_to_all x1, waiting for transfers between devices, per_device(): lax.all_to_all(queries, 'seq', split_axis=1, concat_axis=0, tiled=True)  65.8 us
    psum x1, blocking collectives, per_device(): reduced_rows = lax.psum(reduced_piece.astype(jnp.bfloat16), 'seq')  64.5 us
    psum x1, blocking collectives, per_device(): lax.psum(reduced_gradient_piece.astype(jnp.bfloat16), 'seq')  63.3 us
    sub x2, other arithmetic, attend(): weights = jnp.exp(scores - row_max)  35.3 us
    all_to_all x1, waiting for transfers between devices, per_device(): lax.all_to_all(head_gated, 'seq', split_axis=0, concat_axis=1, tiled=True)  21 us
    dot_general x2, matrix products, attend(): jnp.einsum('gnm,md->ngd', score_grad, key_rows[0], preferred_element_type...  20.5 us
    dot_general x2, matrix products, attend(): jnp.einsum('ngd,md->gnm', query_block, key_rows[0], preferred_element_typ...  16.1 us
  transfers between devices with their start and end apart: 8, of which 3 were waited for; matrix products, arithmetic and copies ran while one was open for 14% of the time, Pallas kernels for 0%

commit v1 on v0

v1 whole, which is shorter than its diff:
```python
import functools

import jax
import jax.numpy as jnp
from jax import lax
from jax.experimental import pallas as pl
from jax.experimental.pallas import tpu as pltpu
from jax.sharding import PartitionSpec as P

EPS = 1e-05
ADAPTER_SCALE = 2.0
MASKED = -1e30
LANES = 128
LOG2_E = 1.4426950408889634
MESH = pl.DeviceIdType.MESH
NT = (((1,), (1,)), ((), ()))
TN = (((0,), (0,)), ((), ()))


def remote(src, dst, send_sem, recv_sem, target):
    return pltpu.make_async_remote_copy(
        src_ref=src,
        dst_ref=dst,
        send_sem=send_sem,
        recv_sem=recv_sem,
        device_id=target,
        device_id_type=MESH,
    )


def loop(first, last, body):
    def step(i, carry):
        body(i)
        return carry

    lax.fori_loop(first, last, step, 0)


def greet(barrier, target):
    pl.semaphore_signal(barrier, inc=1, device_id=target, device_id_type=MESH)


def project_kernel(
    n_dp,
    n_seq,
    docs,
    tiles_ref,
    wk_ref,
    wv_ref,
    wd_ref,
    up_ref,
    gain_ref,
    reader_ref,
    doc_ref,
    kv_ref,
    ext_ref,
    up_all_ref,
    own_k,
    own_v,
    sum_k,
    sum_v,
    low_own,
    low_send,
    low_recv,
    up_recv,
    pick,
    tag,
    rows_buf,
    out_buf,
    in_buf,
    k_ss,
    k_rs,
    v_ss,
    v_rs,
    low_ss,
    low_rs,
    up_ss,
    up_rs,
    out_ss,
    in_rs,
):
    p = lax.axis_index("dp")
    z = lax.axis_index("seq")
    rows = tiles_ref.shape[0]
    rank = up_ref.shape[0]
    img_dev = reader_ref.shape[0]
    img_rows = rows // img_dev
    half, quarter = rows // 2, rows // 4
    right = (p, lax.rem(z + 1, n_seq))
    left = (p, lax.rem(z + n_seq - 1, n_seq))

    def own_part(t):
        ahead = lax.rem(z + 2 * n_seq - 1 - t, n_seq)
        back = lax.rem(z + 1 + t, n_seq)
        for side, head in ((0, ahead), (1, back)):
            cols = pl.ds(pl.multiple_of(head * LANES, LANES), LANES)
            part = pl.ds(side * half, half)
            x = tiles_ref[part, :]
            own_k[part, :] = jnp.dot(x, wk_ref[:, cols], preferred_element_type=jnp.float32)
            own_v[part, :] = jnp.dot(x, wv_ref[:, cols], preferred_element_type=jnp.float32)

    def hop(t, s):
        target = right if s < 2 else left
        part = pl.ds(s * quarter, quarter)
        return (
            remote(sum_k.at[t, part], sum_k.at[t + 1, part], k_ss.at[t, s], k_rs.at[t, s], target),
            remote(sum_v.at[t, part], sum_v.at[t + 1, part], v_ss.at[t, s], v_rs.at[t, s], target),
        )

    def low_copy(k):
        target = (p, lax.rem(z + k, n_seq))
        return remote(low_send, low_recv.at[k], low_ss.at[k], low_rs.at[k], target)

    def up_copy(k, slot):
        target = (p, lax.rem(z + k, n_seq))
        return remote(up_ref, up_recv.at[slot], up_ss.at[k], up_rs.at[k], target)

    barrier = pltpu.get_barrier_semaphore()
    loop(1, n_seq, lambda k: greet(barrier, (p, lax.rem(z + k, n_seq))))
    loop(1, n_dp, lambda k: greet(barrier, (lax.rem(p + k, n_dp), z)))
    own_part(0)
    sum_k[0] = own_k[...]
    sum_v[0] = own_v[...].astype(jnp.bfloat16)
    pl.semaphore_wait(barrier, n_seq - 1 + n_dp - 1)
    for s in (0, 2, 1, 3):
        for copy in hop(0, s):
            copy.start()

    low_part = jnp.dot(tiles_ref[...], wd_ref[...], preferred_element_type=jnp.float32)
    low_own[...] = low_part.T
    low_send[...] = low_own[...].astype(jnp.bfloat16)
    loop(1, n_seq, lambda k: low_copy(k).start())
    loop(1, n_seq, lambda k: up_copy(k, z).start())
    up_recv[z] = up_ref[...]

    def find(g):
        at, mark = jnp.int32(0), jnp.int32(docs)
        for i in range(img_dev):
            hit = reader_ref[i] == g
            at = jnp.where(hit, i, at)
            mark = jnp.where(hit, doc_ref[i], mark)
        pick[g] = at
        tag[g] = mark

    loop(0, n_dp, find)

    def ring_step(t):
        own_part(t)
        for s in (0, 2, 1, 3):
            part = pl.ds(s * quarter, quarter)
            for copy in hop(t - 1, s):
                copy.wait_recv()
            sum_k[t, part, :] = sum_k[t, part, :] + own_k[part, :]
            total_v = sum_v[t, part, :].astype(jnp.float32) + own_v[part, :]
            sum_v[t, part, :] = total_v.astype(jnp.bfloat16)
            for copy in hop(t, s):
                copy.start()

    loop(1, n_seq - 1, ring_step)
    own_part(n_seq - 1)

    low_total = low_own[...]
    for k in range(1, n_seq):
        low_copy(k).wait_recv()
        low_total = low_total + low_recv[k].astype(jnp.float32)
    low_rank = low_total.astype(jnp.bfloat16)
    eye = lax.broadcasted_iota(jnp.int32, (rank, LANES), 0) == lax.broadcasted_iota(
        jnp.int32, (rank, LANES), 1
    )
    eye = jnp.where(eye, 1.0, 0.0).astype(jnp.bfloat16)
    low_up = lax.dot_general(low_rank, up_ref[...], TN, preferred_element_type=jnp.float32)
    low_rows = lax.dot_general(low_rank, eye, TN, preferred_element_type=jnp.float32)
    rows_buf[:, :, 2 * LANES :] = low_rows.astype(jnp.bfloat16).reshape(img_dev, img_rows, LANES)
    own_v[...] = own_v[...] + ADAPTER_SCALE * low_up

    for s in (0, 2, 1, 3):
        part = pl.ds(s * quarter, quarter)
        for copy in hop(n_seq - 2, s):
            copy.wait_recv()
        key_raw = sum_k[n_seq - 1, part, :] + own_k[part, :]
        mean_square = jnp.mean(key_raw * key_raw, axis=-1, keepdims=True)
        key_rows = key_raw * lax.rsqrt(mean_square + EPS) * gain_ref[...]
        images = pl.ds(s * (img_dev // 4), img_dev // 4)
        shape = (img_dev // 4, img_rows, LANES)
        rows_buf[images, :, :LANES] = key_rows.astype(jnp.bfloat16).reshape(shape)
        value = sum_v[n_seq - 1, part, :].astype(jnp.float32) + own_v[part, :]
        rows_buf[images, :, LANES : 2 * LANES] = value.astype(jnp.bfloat16).reshape(shape)

    def image_copy(k, slot):
        g = lax.rem(p + k, n_dp)
        return remote(out_buf.at[g], in_buf.at[slot], out_ss.at[k], in_rs.at[k], (g, z))

    lane = lax.broadcasted_iota(jnp.int32, (img_rows, LANES), 1)

    def image_block(g):
        block = rows_buf[pick[g]]
        mark = jnp.where(lane == rank + tag[g], 1.0, 0.0)
        extra = jnp.where(lane < rank, block[:, 2 * LANES :].astype(jnp.float32), mark)
        return block[:, : 2 * LANES], extra.astype(jnp.bfloat16)

    def send_image(k):
        g = lax.rem(p + k, n_dp)
        kv, extra = image_block(g)
        out_buf[g, :, : 2 * LANES] = kv
        out_buf[g, :, 2 * LANES :] = extra
        image_copy(k, p).start()

    loop(1, n_dp, send_image)
    kv, extra = image_block(p)
    own_rows = pl.ds(pl.multiple_of(p * img_rows, img_rows), img_rows)
    kv_ref[own_rows, :] = kv
    ext_ref[own_rows, :] = extra

    def take_image(k):
        source = lax.rem(p + n_dp - k, n_dp)
        image_copy(k, source).wait_recv()
        into = pl.ds(pl.multiple_of(source * img_rows, img_rows), img_rows)
        kv_ref[into, :] = in_buf[source, :, : 2 * LANES]
        ext_ref[into, :] = in_buf[source, :, 2 * LANES :]

    def take_up(k):
        up_copy(k, lax.rem(z + n_seq - k, n_seq)).wait_recv()

    loop(1, n_seq, take_up)
    up_all_ref[...] = up_recv[...]
    loop(1, n_dp, take_image)

    def sent(t):
        for s in range(4):
            for copy in hop(t, s):
                copy.wait_send()

    loop(0, n_seq - 1, sent)
    loop(1, n_seq, lambda k: low_copy(k).wait_send())
    loop(1, n_seq, lambda k: up_copy(k, z).wait_send())
    loop(1, n_dp, lambda k: image_copy(k, p).wait_send())


def project(n_dp, n_seq, docs, tiles, wk, wv, wd, up, gain, reader, doc):
    rows = tiles.shape[0]
    img_rows = rows // reader.shape[0]
    rank = up.shape[0]
    keys = n_dp * img_rows
    vmem = pl.BlockSpec(memory_space=pltpu.VMEM)
    smem = pl.BlockSpec(memory_space=pltpu.SMEM)
    f32, bf16, dma = jnp.float32, jnp.bfloat16, pltpu.SemaphoreType.DMA
    return pl.pallas_call(
        functools.partial(project_kernel, n_dp, n_seq, docs),
        out_shape=(
            jax.ShapeDtypeStruct((keys, 2 * LANES), bf16),
            jax.ShapeDtypeStruct((keys, LANES), bf16),
            jax.ShapeDtypeStruct((n_seq, rank, LANES), bf16),
        ),
        in_specs=[vmem] * 6 + [smem] * 2,
        out_specs=(vmem, vmem, vmem),
        scratch_shapes=[
            pltpu.VMEM((rows, LANES), f32),
            pltpu.VMEM((rows, LANES), f32),
            pltpu.VMEM((n_seq, rows, LANES), f32),
            pltpu.VMEM((n_seq, rows, LANES), bf16),
            pltpu.VMEM((rank, rows), f32),
            pltpu.VMEM((rank, rows), bf16),
            pltpu.VMEM((n_seq, rank, rows), bf16),
            pltpu.VMEM((n_seq, rank, LANES), bf16),
            pltpu.SMEM((n_dp,), jnp.int32),
            pltpu.SMEM((n_dp,), jnp.int32),
            pltpu.VMEM((reader.shape[0], img_rows, 3 * LANES), bf16),
            pltpu.VMEM((n_dp, img_rows, 3 * LANES), bf16),
            pltpu.VMEM((n_dp, img_rows, 3 * LANES), bf16),
            dma((n_seq, 4)),
            dma((n_seq, 4)),
            dma((n_seq, 4)),
            dma((n_seq, 4)),
            dma((n_seq,)),
            dma((n_seq,)),
            dma((n_seq,)),
            dma((n_seq,)),
            dma((n_dp,)),
            dma((n_dp,)),
        ],
        compiler_params=pltpu.CompilerParams(
            collective_id=0, has_side_effects=True, vmem_limit_bytes=40 << 20
        ),
    )(tiles, wk, wv, wd, up, gain, reader, doc)


def attend_kernel(
    n_seq,
    docs,
    query_hbm,
    grad_hbm,
    kv_hbm,
    ext_ref,
    up_ref,
    gate_ref,
    length_ref,
    gated_hbm,
    query_grad_hbm,
    small_ref,
    query,
    grad,
    gated,
    query_grad,
    kvs,
    bias,
    load_sem,
    store_sem,
    ring_ss,
    ring_rs,
):
    p = lax.axis_index("dp")
    z = lax.axis_index("seq")
    tokens = query.shape[0]
    rank = up_ref.shape[1]
    keys = ext_ref.shape[0]
    width = query.shape[1] // n_seq
    pair = 2 * LANES
    last = n_seq // 2 - 1
    half = keys // 2
    scale = LANES ** (-0.5)
    right = (p, lax.rem(z + 1, n_seq))
    left = (p, lax.rem(z + n_seq - 1, n_seq))

    def ahead(t, b):
        part = pl.ds(b * half, half)
        source, into = lax.rem(n_seq - t, n_seq), n_seq - 1 - t
        return remote(
            kvs.at[source, part], kvs.at[into, part], ring_ss.at[0, t, b], ring_rs.at[0, t, b], right
        )

    def back(t, b):
        part = pl.ds(b * half, half)
        return remote(
            kvs.at[t, part], kvs.at[t + 1, part], ring_ss.at[1, t, b], ring_rs.at[1, t, b], left
        )

    load_kv = pltpu.make_async_copy(kv_hbm, kvs.at[0], load_sem.at[0])
    load_query = pltpu.make_async_copy(query_hbm, query, load_sem.at[1])
    load_grad = pltpu.make_async_copy(grad_hbm, grad, load_sem.at[2])
    load_kv.start()
    barrier = pltpu.get_barrier_semaphore()
    greet(barrier, right)
    greet(barrier, left)
    load_query.start()
    load_grad.start()
    load_kv.wait()
    pl.semaphore_wait(barrier, 2)
    for b in (0, 1):
        if last > 0 or b == 0:
            ahead(0, b).start()
        if last > 0 or b == 1:
            back(0, b).start()

    lane = lax.broadcasted_iota(jnp.int32, (tokens, LANES), 1)
    place = lax.broadcasted_iota(jnp.int32, (tokens, LANES), 0) + z * tokens
    own_doc = jnp.zeros((tokens, LANES), jnp.int32)
    end = jnp.int32(0)
    for d in range(docs - 1):
        end = end + length_ref[0, d]
        own_doc = own_doc + jnp.where(place >= end, 1, 0)
    other = (lane >= rank) & (lane <= rank + docs) & (lane != rank + own_doc)
    penalty = jnp.where(other, MASKED, 0.0).astype(jnp.bfloat16)
    bias[:tokens, :] = penalty
    bias[tokens:, :] = penalty
    small_ref[...] = jnp.zeros_like(small_ref)
    gate = jnp.tanh(jnp.full((1, LANES), gate_ref[0], jnp.float32))
    load_query.wait()
    load_grad.wait()

    def stack(ref, cols):
        both = ref[:, cols]
        return jnp.concatenate([both[:, :LANES], both[:, LANES:]], axis=0)

    def unstack(x):
        return jnp.concatenate([x[:tokens], x[tokens:]], axis=1)

    def attend_pair(slot, head, j):
        cols = pl.ds(pl.multiple_of(head * width + j * pair, pair), pair)
        own_cols = pl.ds(pl.multiple_of(head * LANES, LANES), LANES)
        q = jnp.concatenate([stack(query, cols), bias[...]], axis=1)
        g = (gate * stack(grad, cols).astype(jnp.float32)).astype(jnp.bfloat16)
        key = kvs[slot, :, :LANES]
        value = kvs[slot, :, LANES:]
        extra = ext_ref[...]
        scores = lax.dot_general(
            q, jnp.concatenate([key, extra], axis=1), NT, preferred_element_type=jnp.float32
        )
        prob_grad = lax.dot_general(g, value, NT, preferred_element_type=jnp.float32)
        row_max = jnp.max(scores, axis=1, keepdims=True)
        weights = jnp.exp2((scores - row_max) * (scale * LOG2_E))
        prob = weights * (1.0 / jnp.sum(weights, axis=1, keepdims=True))
        prob_bf16 = prob.astype(jnp.bfloat16)
        attended = jnp.dot(
            prob_bf16, jnp.concatenate([value, extra], axis=1), preferred_element_type=jnp.float32
        )
        low_seen = attended[:, LANES : LANES + rank].astype(jnp.bfloat16)
        attended = attended[:, :LANES]
        gated[:, cols] = unstack((gate * attended).astype(jnp.bfloat16))
        delta = jnp.sum(g.astype(jnp.float32) * attended, axis=1, keepdims=True)
        score_grad = (prob * (prob_grad - delta)).astype(jnp.bfloat16)
        out_grad = jnp.dot(score_grad, key, preferred_element_type=jnp.float32) * scale
        query_grad[:, cols] = unstack(out_grad.astype(jnp.bfloat16))
        grad_up = lax.dot_general(up_ref[head], g, NT, preferred_element_type=jnp.float32)
        small_ref[:rank, :] += jnp.dot(
            grad_up.astype(jnp.bfloat16), prob_bf16, preferred_element_type=jnp.float32
        )
        small_ref[rank:, own_cols] += lax.dot_general(
            low_seen, g, TN, preferred_element_type=jnp.float32
        )

    def store(i, head):
        cols = pl.ds(pl.multiple_of(head * width, width), width)
        return (
            pltpu.make_async_copy(gated.at[:, cols], gated_hbm.at[:, cols], store_sem.at[0, i]),
            pltpu.make_async_copy(
                query_grad.at[:, cols], query_grad_hbm.at[:, cols], store_sem.at[1, i]
            ),
        )

    def slot_of(i):
        return jnp.where(lax.rem(i, 2) == 1, n_seq - (i + 1) // 2, i // 2)

    def head_step(i):
        step = (i + 1) // 2
        arrives = lax.rem(i, 2) == 1

        @pl.when(arrives & (step <= last))
        def _():
            for b in (0, 1):
                ahead(step - 1, b).wait_recv()
                if b == 0:
                    ahead(step, b).start()
                else:
                    pl.when(step < last)(lambda: ahead(step, 1).start())
                back(step - 1, b).wait_recv()
                if b == 1:
                    back(step, b).start()
                else:
                    pl.when(step < last)(lambda: back(step, 0).start())

        @pl.when(i == n_seq - 1)
        def _():
            ahead(last, 0).wait_recv()
            back(last, 1).wait_recv()

        slot = slot_of(i)
        head = lax.rem(z + slot, n_seq)
        loop(0, width // pair, lambda j: attend_pair(slot, head, j))
        for copy in store(i, head):
            copy.start()

    loop(0, n_seq, head_step)

    def stored(i):
        for copy in store(i, lax.rem(z + slot_of(i), n_seq)):
            copy.wait()

    loop(0, n_seq, stored)
    for t in range(last + 1):
        for b in (0, 1):
            if t < last or b == 0:
                ahead(t, b).wait_send()
            if t < last or b == 1:
                back(t, b).wait_send()


def attend(n_seq, docs, queries, grads, kv, ext, up_all, gate, lengths):
    tokens, columns = queries.shape
    keys = kv.shape[0]
    rank = up_all.shape[1]
    any_space = pl.BlockSpec(memory_space=pl.ANY)
    vmem = pl.BlockSpec(memory_space=pltpu.VMEM)
    smem = pl.BlockSpec(memory_space=pltpu.SMEM)
    f32, bf16, dma = jnp.float32, jnp.bfloat16, pltpu.SemaphoreType.DMA
    wide = pltpu.VMEM((tokens, columns), bf16)
    return pl.pallas_call(
        functools.partial(attend_kernel, n_seq, docs),
        out_shape=(
            jax.ShapeDtypeStruct((tokens, columns), bf16),
            jax.ShapeDtypeStruct((tokens, columns), bf16),
            jax.ShapeDtypeStruct((2 * rank, keys), f32),
        ),
        in_specs=[any_space] * 3 + [vmem] * 2 + [smem] * 2,
        out_specs=(any_space, any_space, vmem),
        scratch_shapes=[
            wide,
            wide,
            wide,
            wide,
            pltpu.VMEM((n_seq, keys, 2 * LANES), bf16),
            pltpu.VMEM((2 * tokens, LANES), bf16),
            dma((3,)),
            dma((2, n_seq)),
            dma((2, n_seq // 2, 2)),
            dma((2, n_seq // 2, 2)),
        ],
        compiler_params=pltpu.CompilerParams(
            collective_id=1, has_side_effects=True, vmem_limit_bytes=48 << 20
        ),
    )(queries, grads, kv, ext, up_all, gate, lengths)


def adapter_kernel(
    n_dp,
    n_seq,
    rank,
    small_ref,
    tiles_ref,
    reader_ref,
    down_ref,
    up_ref,
    col_recv,
    low_send,
    low_recv,
    total,
    sum_recv,
    done,
    col_ss,
    col_rs,
    low_ss,
    low_rs,
    sum_ss,
    sum_rs,
    done_ss,
    done_rs,
):
    p = lax.axis_index("dp")
    z = lax.axis_index("seq")
    rows, width = tiles_ref.shape
    img_dev = reader_ref.shape[0]
    img_rows = rows // img_dev
    fit = LANES // img_rows
    wide = total.shape[1]
    pieces = 2 * (wide // LANES)

    def sends_to(n):
        return fit * z + lax.rem(n, fit), n // fit

    barrier = pltpu.get_barrier_semaphore()
    loop(1, n_seq, lambda k: greet(barrier, (p, lax.rem(z + k, n_seq))))
    loop(1, n_dp, lambda k: greet(barrier, (lax.rem(p + k, n_dp), z)))
    owner = p // fit

    def greet_sender(k):
        g = lax.rem(p + k, n_dp)

        @pl.when((k != 0) | (owner != z))
        def _():
            greet(barrier, (g, owner))

    loop(0, n_dp, greet_sender)
    pl.semaphore_wait(barrier, n_seq - 1 + n_dp - 1 + n_dp - jnp.where(owner == z, 1, 0))

    def col_copy(k):
        target = lax.rem(z + k, n_seq)
        cols = pl.ds(pl.multiple_of(target * LANES, LANES), LANES)
        return remote(
            small_ref.at[:, cols], col_recv.at[k], col_ss.at[k], col_rs.at[k], (p, target)
        )

    loop(1, n_seq, lambda k: col_copy(k).start())
    own = small_ref[:, pl.ds(pl.multiple_of(z * LANES, LANES), LANES)]
    for k in range(1, n_seq):
        col_copy(k).wait_recv()
        own = own + col_recv[k]
    own = ADAPTER_SCALE * own
    low_send[...] = own[:rank].astype(jnp.bfloat16)
    total[:, width:] = jnp.zeros((rank, wide - width), jnp.float32)
    total[:, wide - LANES :] = own[rank:]

    def low_copy(n, slot):
        o, s = sends_to(n)
        return remote(low_send, low_recv.at[slot], low_ss.at[n], low_rs.at[p], (o, s))

    def low_start(n):
        o, s = sends_to(n)
        mine = (o == p) & (s == z)

        @pl.when(mine)
        def _():
            low_recv[p] = low_send[...]

        @pl.when(jnp.logical_not(mine))
        def _():
            low_copy(n, p).start()

    loop(0, fit * n_seq, low_start)

    def low_wait(g):
        @pl.when((g != p) | (owner != z))
        def _():
            remote(
                low_send, low_recv.at[g], low_ss.at[0], low_rs.at[g], (g, owner)
            ).wait_recv()

    loop(0, n_dp, low_wait)

    lane = lax.broadcasted_iota(jnp.int32, (rank, LANES), 1)
    held = lax.rem(p, fit)
    for first in range(0, img_dev, fit):
        piece = jnp.zeros((rank, LANES), jnp.float32)
        for i in range(fit):
            block = low_recv[reader_ref[first + i]].astype(jnp.float32)
            shift = lax.rem(i - held + fit, fit) * img_rows
            block = pltpu.roll(block, shift, 1)
            piece = jnp.where(lane // img_rows == i, block, piece)
        part = jnp.dot(
            piece.astype(jnp.bfloat16),
            tiles_ref[first * img_rows : (first + fit) * img_rows, :],
            preferred_element_type=jnp.float32,
        )
        if first == 0:
            total[:, :width] = part
        else:
            total[:, :width] += part

    def piece_of(ref, j):
        return ref.at[
            pl.ds(pl.multiple_of(lax.rem(j, 2) * 8, 8), 8),
            pl.ds(pl.multiple_of((j // 2) * LANES, LANES), LANES),
        ]

    def sum_copy(j):
        k = lax.rem(j - p + n_dp, n_dp)
        return remote(
            piece_of(total, j), sum_recv.at[k], sum_ss.at[j], sum_rs.at[k], (j, z)
        )

    loop(0, pieces, lambda j: pl.when(j != p)(lambda: sum_copy(j).start()))

    def done_copy(k, j):
        g = lax.rem(p + k, n_dp)
        return remote(done.at[j], done.at[j], done_ss.at[k], done_rs.at[j], (g, z))

    @pl.when(p < pieces)
    def _():
        def take(k, acc):
            remote(
                piece_of(total, p), sum_recv.at[k], sum_ss.at[0], sum_rs.at[k], (p, z)
            ).wait_recv()
            return acc + sum_recv[k]

        done[p] = lax.fori_loop(1, n_dp, take, piece_of(total, p)[...])
        loop(1, n_dp, lambda k: done_copy(k, p).start())

    loop(0, pieces, lambda j: pl.when(j != p)(lambda: done_copy(0, j).wait_recv()))
    for j in range(pieces - 2):
        r, c = 8 * (j % 2), LANES * (j // 2)
        fill = min(LANES, width - c)
        if fill > 0:
            down_ref[r : r + 8, c : c + fill] = done[j][:, :fill]
    up_ref[:8, :] = done[pieces - 2]
    up_ref[8:, :] = done[pieces - 1]

    loop(1, n_seq, lambda k: col_copy(k).wait_send())

    def low_sent(n):
        o, s = sends_to(n)

        @pl.when((o != p) | (s != z))
        def _():
            low_copy(n, p).wait_send()

    loop(0, fit * n_seq, low_sent)
    loop(0, pieces, lambda j: pl.when(j != p)(lambda: sum_copy(j).wait_send()))

    @pl.when(p < pieces)
    def _():
        loop(1, n_dp, lambda k: done_copy(k, p).wait_send())


def adapter(n_dp, n_seq, rank, small, tiles, reader):
    rows, width = tiles.shape
    wide = -(-width // LANES) * LANES + LANES
    pieces = 2 * (wide // LANES)
    img_rows = rows // reader.shape[0]
    vmem = pl.BlockSpec(memory_space=pltpu.VMEM)
    smem = pl.BlockSpec(memory_space=pltpu.SMEM)
    f32, bf16, dma = jnp.float32, jnp.bfloat16, pltpu.SemaphoreType.DMA
    fan = (LANES // img_rows) * n_seq
    return pl.pallas_call(
        functools.partial(adapter_kernel, n_dp, n_seq, rank),
        out_shape=(
            jax.ShapeDtypeStruct((rank, width), f32),
            jax.ShapeDtypeStruct((rank, LANES), f32),
        ),
        in_specs=[vmem, vmem, smem],
        out_specs=(vmem, vmem),
        scratch_shapes=[
            pltpu.VMEM((n_seq, 2 * rank, LANES), f32),
            pltpu.VMEM((rank, LANES), bf16),
            pltpu.VMEM((n_dp, rank, LANES), bf16),
            pltpu.VMEM((rank, wide), f32),
            pltpu.VMEM((n_dp, 8, LANES), f32),
            pltpu.VMEM((pieces, 8, LANES), f32),
            dma((n_seq,)),
            dma((n_seq,)),
            dma((fan,)),
            dma((n_dp,)),
            dma((pieces,)),
            dma((n_dp,)),
            dma((n_dp,)),
            dma((pieces,)),
        ],
        compiler_params=pltpu.CompilerParams(
            collective_id=2, has_side_effects=True, vmem_limit_bytes=16 << 20
        ),
    )(small, tiles, reader)


def per_device(
    queries,
    output_gradient,
    tiles,
    frozen_key_weight,
    frozen_value_weight,
    key_norm_gain,
    adapter_down_weight,
    adapter_up_weight,
    gate,
    document_lengths,
    image_reader_group,
    image_document,
):
    n_dp, n_seq = lax.axis_size("dp"), lax.axis_size("seq")
    docs = document_lengths.shape[1]
    rank = adapter_up_weight.shape[0]
    img_dev, img_rows, width = tiles.shape
    flat_tiles = tiles.reshape(img_dev * img_rows, width)
    kv, ext, up_all = project(
        n_dp,
        n_seq,
        docs,
        flat_tiles,
        frozen_key_weight,
        frozen_value_weight,
        adapter_down_weight,
        adapter_up_weight,
        key_norm_gain.reshape(1, -1),
        image_reader_group,
        image_document,
    )
    gated, query_grad, small = attend(
        n_seq, docs, queries, output_gradient, kv, ext, up_all, gate, document_lengths
    )
    down_rows, up_grad = adapter(n_dp, n_seq, rank, small, flat_tiles, image_reader_group)
    return (gated, query_grad, down_rows.T, up_grad)


def solution(mesh):
    placed = (
        P(("dp", "seq"), None),
        P(("dp", "seq"), None),
        P("dp", None, "seq"),
        P("seq", None),
        P("seq", None),
        P(),
        P("seq", None),
        P(None, "seq"),
        P(),
        P("dp", None),
        P("dp"),
        P("dp"),
    )
    return jax.shard_map(
        per_device,
        mesh=mesh,
        in_specs=placed,
        out_specs=(P(("dp", "seq"), None), P(("dp", "seq"), None), P("seq", None), P(None, "seq")),
        check_vma=False,
    )
```

time: 591 us -> 163 us (0.28); the launches traced: 581 us -> 162 us
  blocking collectives: 254 us -> 0 us
  Pallas kernels: 0 us -> 149 us
  waiting for transfers between devices: 90.5 us -> 0 us
  other arithmetic: 65.1 us -> 0 us
  matrix products: 57 us -> 0 us
  starting transfers between devices: 49 us -> 0 us
  local copies, waits for them, and re-layouts: 49.8 us -> 11.8 us
  between operations: 15.3 us -> 1.36 us
    psum x3 -> x0, blocking collectives: 254 us -> none  [the longest x1 126 us: per_device(): lax.psum(down_part.astype(jnp.bfloat16), 'dp').astype(jnp.float32)]
    pallas_call x0 -> x3, Pallas kernels: none -> 149 us  [the longest x1 59 us: project(): pl.pallas_call(functools.partial(project_kernel, n_dp, n_seq, docs), out_...]
    all_to_all x7 -> x0, waiting for transfers between devices: 90.5 us -> none  [the longest x1 65.8 us: per_device(): lax.all_to_all(queries, 'seq', split_axis=1, concat_axis=0, tiled=True)]
    dot_general x18 -> x0, matrix products: 57 us -> none  [the longest x2 20.5 us: attend(): jnp.einsum('gnm,md->ngd', score_grad, key_rows[0], preferred_element_type...]
    all_to_all x7 -> x0, starting transfers between devices: 48.9 us -> none  [the longest x1 10.8 us: per_device(): lax.all_to_all(outgoing, 'dp', split_axis=0, concat_axis=0, tiled=True)]
    sub x2 -> x0, other arithmetic: 35.3 us -> none  [attend(): weights = jnp.exp(scores - row_max)]
    convert_element_type x7 -> x0, other arithmetic: 20.3 us -> none  [the longest x2 14 us: attend(): prob_bf16 = prob_f32.astype(jnp.bfloat16)]
    all_to_all x4 -> x0, local copies, waits for them, and re-layouts: 11.7 us -> none  [the longest x1 3.9 us: per_device(): lax.all_to_all(head_gated, 'seq', split_axis=0, concat_axis=1, tiled=True)]
  transfers between devices with their start and end apart: 8 -> 0, of which waited for: 3 -> 0; matrix products, arithmetic and copies ran while one was open for 14% -> 0% of each run, Pallas kernels for 0% -> 0%
where the time goes in v1:
time: 163 us; the launch traced here: 162 us
  Pallas kernels  149 us (91%)
  local copies, waits for them, and re-layouts  11.8 us (7%)
    pallas_call x1, Pallas kernels, project(): pl.pallas_call(functools.partial(project_kernel, n_dp, n_seq, docs), out_...  59 us
    pallas_call x1, Pallas kernels, attend(): pl.pallas_call(functools.partial(attend_kernel, n_seq, docs), out_shape=(...  55.8 us
    pallas_call x1, Pallas kernels, adapter(): pl.pallas_call(functools.partial(adapter_kernel, n_dp, n_seq, rank), out_...  34.3 us
    unnamed x25, local copies, waits for them, and re-layouts  11.8 us

profile of v1, /device:TPU:1, one launch (start us, length us, event | category | flops | bytes accessed | tf_op | source)
XLA Modules:
  0.0 162.2 jit_solution(12203813179079223659)
XLA Ops:
  0.6 0.9 copy.16.wd_ref
  1.6 0.0 copy-start
  1.6 1.2 copy-done
  2.8 0.0 copy-start.2
  2.8 1.5 copy-done.2
  4.4 0.0 copy-start.3
  4.4 1.5 copy-done.3
  5.9 0.0 copy-start.4
  5.9 0.7 copy-done.4
  6.6 0.0 copy-start.5
  6.6 0.7 copy-done.5
  7.2 0.0 copy-start.8
  7.2 0.7 copy-done.8
  7.9 0.0 copy-start.9
  7.9 0.7 copy-done.9
  8.6 0.0 copy-start.7
  8.6 59.0 %shard_map.147 = (bf16[1024,256]{1,0:T(8,128)(2,1)S(1)}, bf16[1024,128]{1,0:T(8,128)(2,1)S(1)}, bf16[8,16,128]{2,1,0:T(8,128)(2,1)S(1)}) custom-call(bf16[512,960]{1,0:T(8,128)(2,1)S(1)} %bitcast.3, bf16[960,1024]{1,0:T(8,128)(2,1)S(1)} %copy-done.2, bf16[960,1024]{1,0:T(8,128)(2,1)S(1)} %copy-done.3, bf16[960,16]{1,0:T(8,128)(2,1)S(1)} %copy.16.wd_ref, ...), custom_call_target="tpu_custom_call" | custom-call | tf_op jit(solution)/shard_map/pallas_call | solution.py:247
  68.2 0.0 copy-done.7
  68.2 0.0 copy-start.1
  68.2 0.0 copy-start.6
  68.2 55.8 %shard_map.148 = (bf16[128,8192]{1,0:T(8,128)(2,1)S(1)}, bf16[128,8192]{1,0:T(8,128)(2,1)S(1)}, f32[32,1024]{1,0:T(8,128)S(1)}) custom-call(bf16[128,8192]{1,0:T(8,128)(2,1)} %query_hbm.1, bf16[128,8192]{1,0:T(8,128)(2,1)} %grad_hbm.1, bf16[1024,256]{1,0:T(8,128)(2,1)S(1)} %get-tuple-element.12.kv_hbm, bf16[1024,128]{1,0:T(8,128)(2,1)S(1)} %get-tuple-element.13.ext_ref, ...), custom_call_target="tpu_custom_call" | custom-call | tf_op jit(solution)/shard_map/pallas_call | solution.py:476
  124.1 0.0 copy-done.1
  124.1 0.0 copy-done.6
  124.1 34.3 %shard_map.149 = (f32[16,960]{1,0:T(8,128)S(1)}, f32[16,128]{1,0:T(8,128)S(1)}) custom-call(f32[32,1024]{1,0:T(8,128)S(1)} %get-tuple-element.17.small_ref, bf16[512,960]{1,0:T(8,128)(2,1)S(1)} %bitcast.4, s32[16]{0:T(128)S(1)} %copy-done.6), custom_call_target="tpu_custom_call" | custom-call | tf_op jit(solution)/shard_map/pallas_call | solution.py:681
  158.4 1.3 copy.22
  159.7 1.3 copy.23
  161.0 0.6 copy.24
  161.6 0.6 copy.25
Async XLA Ops:
  1.6 1.2 copy-start
  2.8 1.5 copy-start.2
  4.4 1.5 copy-start.3
  5.9 0.7 copy-start.4
  6.6 0.7 copy-start.5
  7.2 0.7 copy-start.8
  7.9 0.7 copy-start.9
  8.6 59.7 %copy-start.7 = (s32[1,4]{1,0:T(1,128)S(1)}, s32[1,4]{1,0:T(1,128)}, u32[]{:S(2)}) copy-start(s32[1,4]{1,0:T(1,128)} %length_ref.1) | copy-start | bytes 52
  68.2 55.9 %copy-start.1 = (bf16[16,32,960]{2,1,0:T(8,128)(2,1)S(1)}, bf16[16,32,960]{2,1,0:T(8,128)(2,1)}, u32[]{:S(2)}) copy-start(bf16[16,32,960]{2,1,0:T(8,128)(2,1)} %param.14) | copy-start | bytes 2949124
  68.2 55.9 %copy-start.6 = (s32[16]{0:T(128)S(1)}, s32[16]{0:T(128)}, u32[]{:S(2)}) copy-start(s32[16]{0:T(128)} %reader_ref.3) | copy-start | bytes 196

commit v2 on v0

v2 whole, which is shorter than its diff:
```python
import functools

import jax
import jax.numpy as jnp
from jax import lax
from jax.experimental import pallas as pl
from jax.experimental.pallas import tpu as pltpu
from jax.sharding import PartitionSpec as P

EPS = 1e-05
ADAPTER_SCALE = 2.0
MASKED = -1e30
LANES = 128
CHUNK = 64
PARTS = 4
HEADS_AT_ONCE = 4
LOG2_E = 1.4426950408889634
MESH = pl.DeviceIdType.MESH
NT = (((1,), (1,)), ((), ()))
TN = (((0,), (0,)), ((), ()))


def remote(src, dst, send_sem, recv_sem, target):
    return pltpu.make_async_remote_copy(
        src_ref=src,
        dst_ref=dst,
        send_sem=send_sem,
        recv_sem=recv_sem,
        device_id=target,
        device_id_type=MESH,
    )


def loop(first, last, body):
    def step(i, carry):
        body(i)
        return carry

    lax.fori_loop(first, last, step, 0)


def greet(barrier, target):
    pl.semaphore_signal(barrier, inc=1, device_id=target, device_id_type=MESH)


def fused_kernel(
    n_dp,
    n_seq,
    docs,
    query_hbm,
    grad_hbm,
    tiles_hbm,
    wk_hbm,
    wv_hbm,
    wd_hbm,
    up_ref,
    gain_ref,
    gate_ref,
    length_ref,
    reader_ref,
    doc_ref,
    gated_hbm,
    query_grad_hbm,
    down_ref,
    up_out_ref,
    query,
    grad,
    gated,
    query_grad,
    tiles,
    wk,
    wv,
    wd,
    own_k,
    own_v,
    sum_k,
    sum_v,
    low_own,
    low_out,
    low_in,
    up_all,
    pick,
    tag,
    rows_buf,
    ext_rows,
    kv_out,
    ext_out,
    kvs,
    ext,
    bias,
    prob_buf,
    delta_buf,
    small,
    col_in,
    back_out,
    back_in,
    total,
    sum_in,
    done,
    load_sem,
    store_sem,
    k_ss,
    k_rs,
    v_ss,
    v_rs,
    low_ss,
    low_rs,
    up_ss,
    up_rs,
    kv_ss,
    kv_rs,
    ext_ss,
    ext_rs,
    ring_ss,
    ring_rs,
    col_ss,
    col_rs,
    back_ss,
    back_rs,
    sum_ss,
    sum_rs,
    done_ss,
    done_rs,
):
    p = lax.axis_index("dp")
    z = lax.axis_index("seq")
    rows, width = tiles.shape
    tokens, columns = query.shape
    rank = up_ref.shape[0]
    img_dev = reader_ref.shape[0]
    img_rows = rows // img_dev
    keys = ext.shape[0]
    head_width = columns // n_seq
    block = bias.shape[0]
    fit = LANES // img_rows
    half = rows // 2
    chunks = rows // CHUNK
    scale = LANES ** (-0.5)
    right = (p, lax.rem(z + 1, n_seq))
    left = (p, lax.rem(z + n_seq - 1, n_seq))

    def lanes_of(n, size=LANES):
        return pl.ds(pl.multiple_of(n * size, size), size)

    loads = [
        pltpu.make_async_copy(source, into, load_sem.at[n])
        for n, (source, into) in enumerate(
            (
                (tiles_hbm, tiles),
                (wk_hbm, wk),
                (wv_hbm, wv),
                (wd_hbm, wd),
                (query_hbm, query),
                (grad_hbm, grad),
            )
        )
    ]
    for load in loads:
        load.start()
    barrier = pltpu.get_barrier_semaphore()
    loop(1, n_seq, lambda k: greet(barrier, (p, lax.rem(z + k, n_seq))))
    loop(1, n_dp, lambda k: greet(barrier, (lax.rem(p + k, n_dp), z)))

    def greet_back(k):
        @pl.when((k != 0) | (z != 0))
        def _():
            greet(barrier, (lax.rem(p + k, n_dp), k // fit))

    loop(0, n_dp, greet_back)

    def own_part(t):
        ahead = lax.rem(z + 2 * n_seq - 1 - t, n_seq)
        back = lax.rem(z + 1 + t, n_seq)
        for side, head in ((0, ahead), (1, back)):
            part = pl.ds(side * half, half)
            x = tiles[part, :]
            own_k[part, :] = jnp.dot(x, wk[:, lanes_of(head)], preferred_element_type=jnp.float32)
            own_v[part, :] = jnp.dot(x, wv[:, lanes_of(head)], preferred_element_type=jnp.float32)

    order = [c + side * (chunks // 2) for c in range(chunks // 2) for side in (0, 1)]

    def hop(t, s):
        target = right if s < chunks // 2 else left
        part = pl.ds(s * CHUNK, CHUNK)
        return (
            remote(sum_k.at[t, part], sum_k.at[t + 1, part], k_ss.at[t, s], k_rs.at[t, s], target),
            remote(sum_v.at[t, part], sum_v.at[t + 1, part], v_ss.at[t, s], v_rs.at[t, s], target),
        )

    for load in loads[:3]:
        load.wait()
    own_part(0)
    sum_k[0] = own_k[...]
    sum_v[0] = own_v[...].astype(jnp.bfloat16)
    pl.semaphore_wait(barrier, n_seq - 1 + n_dp - 1 + n_dp - jnp.where(z == 0, 1, 0))
    for s in order:
        for copy in hop(0, s):
            copy.start()

    def low_copy(k):
        target = (p, lax.rem(z + k, n_seq))
        return remote(low_out, low_in.at[k], low_ss.at[k], low_rs.at[k], target)

    def up_copy(k, slot):
        target = (p, lax.rem(z + k, n_seq))
        return remote(up_ref, up_all.at[slot], up_ss.at[k], up_rs.at[k], target)

    loads[3].wait()
    low_own[...] = lax.dot_general(wd[...], tiles[...], NT, preferred_element_type=jnp.float32)
    low_out[...] = low_own[...].astype(jnp.bfloat16)
    loop(1, n_seq, lambda k: low_copy(k).start())
    loop(1, n_seq, lambda k: up_copy(k, z).start())
    up_all[z] = up_ref[...]

    def find(g):
        at, mark = jnp.int32(0), jnp.int32(docs)
        for i in range(img_dev):
            hit = reader_ref[i] == g
            at = jnp.where(hit, i, at)
            mark = jnp.where(hit, doc_ref[i], mark)
        pick[g] = at
        tag[g] = mark

    def kv_copy(k):
        g = lax.rem(p + k, n_dp)
        into = kvs.at[0, pl.ds(pl.multiple_of(k * img_rows, img_rows), img_rows)]
        return remote(kv_out.at[k], into, kv_ss.at[k], kv_rs.at[k], (g, z))

    def ext_copy(k):
        g = lax.rem(p + k, n_dp)
        into = ext.at[pl.ds(pl.multiple_of(k * img_rows, img_rows), img_rows)]
        return remote(ext_out.at[k], into, ext_ss.at[k], ext_rs.at[k], (g, z))

    lane = lax.broadcasted_iota(jnp.int32, (img_rows, LANES), 1)

    def ext_block(g):
        mark = jnp.where(lane == rank + tag[g], 1.0, 0.0)
        low = ext_rows[pick[g]].astype(jnp.float32)
        return jnp.where(lane < rank, low, mark).astype(jnp.bfloat16)

    def send_ext(k):
        ext_out[k] = ext_block(lax.rem(p + k, n_dp))
        ext_copy(k).start()

    def low_finish():
        low_total = low_own[...]
        for k in range(1, n_seq):
            low_copy(k).wait_recv()
            low_total = low_total + low_in[k].astype(jnp.float32)
        low_rank = low_total.astype(jnp.bfloat16)
        low_out[...] = low_rank
        eye = lax.broadcasted_iota(jnp.int32, (rank, LANES), 0) == lax.broadcasted_iota(
            jnp.int32, (rank, LANES), 1
        )
        eye = jnp.where(eye, 1.0, 0.0).astype(jnp.bfloat16)
        low_rows = lax.dot_general(low_rank, eye, TN, preferred_element_type=jnp.float32)
        ext_rows[...] = low_rows.astype(jnp.bfloat16).reshape(img_dev, img_rows, LANES)

    def low_sends():
        loop(1, n_seq, lambda k: low_copy(k).wait_send())

    def ring_step(t):
        own_part(t)
        for s in order:
            part = pl.ds(s * CHUNK, CHUNK)
            for copy in hop(t - 1, s):
                copy.wait_recv()
            sum_k[t, part, :] = sum_k[t, part, :] + own_k[part, :]
            total_v = sum_v[t, part, :].astype(jnp.float32) + own_v[part, :]
            sum_v[t, part, :] = total_v.astype(jnp.bfloat16)
            for copy in hop(t, s):
                copy.start()

    if n_seq > 3:
        loop(0, n_dp, find)
        loop(1, 3, ring_step)
        low_sends()
        low_finish()
        each = -(-(n_dp - 1) // (n_seq - 4))

        def ring_and_ext(t):
            first = 1 + (t - 3) * each
            loop(first, jnp.minimum(first + each, n_dp), send_ext)
            ring_step(t)

        loop(3, n_seq - 1, ring_and_ext)
    else:
        loop(0, n_dp, find)
        loop(1, n_seq - 1, ring_step)
        low_sends()
        low_finish()
        loop(1, n_dp, send_ext)
    ext[:img_rows, :] = ext_block(p)

    own_part(n_seq - 1)
    low_up = lax.dot_general(low_out[...], up_ref[...], TN, preferred_element_type=jnp.float32)
    own_v[...] = own_v[...] + ADAPTER_SCALE * low_up

    lane_tok = lax.broadcasted_iota(jnp.int32, (tokens, LANES), 1)
    place = lax.broadcasted_iota(jnp.int32, (tokens, LANES), 0) + z * tokens
    own_doc = jnp.zeros((tokens, LANES), jnp.int32)
    end = jnp.int32(0)
    for d in range(docs - 1):
        end = end + length_ref[0, d]
        own_doc = own_doc + jnp.where(place >= end, 1, 0)
    other = (lane_tok >= rank) & (lane_tok <= rank + docs) & (lane_tok != rank + own_doc)
    penalty = jnp.where(other, MASKED, 0.0).astype(jnp.bfloat16)
    for n in range(block // tokens):
        bias[n * tokens : (n + 1) * tokens, :] = penalty
    small[...] = jnp.zeros_like(small)
    gate = jnp.tanh(jnp.full((1, LANES), gate_ref[0], jnp.float32))

    per_chunk = CHUNK // img_rows
    for s in order:
        part = pl.ds(s * CHUNK, CHUNK)
        images = pl.ds(s * per_chunk, per_chunk)
        for copy in hop(n_seq - 2, s):
            copy.wait_recv()
        key_raw = sum_k[n_seq - 1, part, :] + own_k[part, :]
        mean_square = jnp.mean(key_raw * key_raw, axis=-1, keepdims=True)
        key_rows = key_raw * lax.rsqrt(mean_square + EPS) * gain_ref[...]
        value = sum_v[n_seq - 1, part, :].astype(jnp.float32) + own_v[part, :]
        both = jnp.concatenate([key_rows, value], axis=1).astype(jnp.bfloat16)
        rows_buf[images] = both.reshape(per_chunk, img_rows, 2 * LANES)

    def send_kv(k):
        kv_out[k] = rows_buf[pick[lax.rem(p + k, n_dp)]]
        kv_copy(k).start()

    loop(1, n_dp, send_kv)
    kvs[0, :img_rows, :] = rows_buf[pick[p]]

    last = n_seq // 2 - 1
    part_rows = keys // PARTS

    def ahead(t, b):
        part = pl.ds(b * part_rows, part_rows)
        source, into = lax.rem(n_seq - t, n_seq), n_seq - 1 - t
        return remote(
            kvs.at[source, part], kvs.at[into, part], ring_ss.at[0, t, b], ring_rs.at[0, t, b], right
        )

    def back(t, b):
        part = pl.ds(b * part_rows, part_rows)
        return remote(
            kvs.at[t, part], kvs.at[t + 1, part], ring_ss.at[1, t, b], ring_rs.at[1, t, b], left
        )

    ways = ((ahead, lambda b: b < PARTS // 2), (back, lambda b: b >= PARTS // 2))
    slots = n_dp // PARTS
    for b in range(PARTS):
        loop(max(1, b * slots), (b + 1) * slots, lambda k: kv_copy(k).wait_recv())
        for way, whole in ways:
            if last > 0 or whole(b):
                way(0, b).start()
    loop(1, n_dp, lambda k: ext_copy(k).wait_recv())
    loop(1, n_seq, lambda k: up_copy(k, lax.rem(z + n_seq - k, n_seq)).wait_recv())
    loads[4].wait()
    loads[5].wait()

    def stack(ref, cols):
        part = ref[:, cols]
        return jnp.concatenate(
            [part[:, n * LANES : (n + 1) * LANES] for n in range(block // tokens)], axis=0
        )

    def unstack(x):
        return jnp.concatenate(
            [x[n * tokens : (n + 1) * tokens] for n in range(block // tokens)], axis=1
        )

    span = (block // tokens) * LANES

    def cols_of(head, j):
        return pl.ds(pl.multiple_of(head * head_width + j * span, span), span)

    def grad_rows(cols):
        return (gate * stack(grad, cols).astype(jnp.float32)).astype(jnp.bfloat16)

    def probabilities(slot, head, j):
        cols = cols_of(head, j)
        q = jnp.concatenate([stack(query, cols), bias[...]], axis=1)
        g = grad_rows(cols)
        key_ext = jnp.concatenate([kvs[slot, :, :LANES], ext[...]], axis=1)
        scores = lax.dot_general(q, key_ext, NT, preferred_element_type=jnp.float32)
        row_max = jnp.max(scores, axis=1, keepdims=True)
        weights = jnp.exp2((scores - row_max) * (scale * LOG2_E))
        prob = weights * (1.0 / jnp.sum(weights, axis=1, keepdims=True))
        prob_bf16 = prob.astype(jnp.bfloat16)
        value_ext = jnp.concatenate([kvs[slot, :, LANES:], ext[...]], axis=1)
        attended = jnp.dot(prob_bf16, value_ext, preferred_element_type=jnp.float32)
        low_seen = attended[:, LANES : LANES + rank].astype(jnp.bfloat16)
        attended = attended[:, :LANES]
        gated[:, cols] = unstack((gate * attended).astype(jnp.bfloat16))
        delta = jnp.sum(g.astype(jnp.float32) * attended, axis=1, keepdims=True)
        grad_up = lax.dot_general(up_all[head], g, NT, preferred_element_type=jnp.float32)
        small[:rank, :] += jnp.dot(
            grad_up.astype(jnp.bfloat16), prob_bf16, preferred_element_type=jnp.float32
        )
        small[rank:, lanes_of(head)] += lax.dot_general(
            low_seen, g, TN, preferred_element_type=jnp.float32
        )
        return g, prob, delta

    def query_gradient(slot, head, j, g, prob, delta):
        prob_grad = lax.dot_general(
            g, kvs[slot, :, LANES:], NT, preferred_element_type=jnp.float32
        )
        score_grad = (prob * (prob_grad - delta)).astype(jnp.bfloat16)
        out_grad = jnp.dot(score_grad, kvs[slot, :, :LANES], preferred_element_type=jnp.float32)
        query_grad[:, cols_of(head, j)] = unstack((out_grad * scale).astype(jnp.bfloat16))

    def store(n, i, head):
        cols = lanes_of(head, head_width)
        source, into = ((gated, gated_hbm), (query_grad, query_grad_hbm))[n]
        return pltpu.make_async_copy(source.at[:, cols], into.at[:, cols], store_sem.at[n, i])

    def slot_of(i):
        return jnp.where(lax.rem(i, 2) == 1, n_seq - (i + 1) // 2, i // 2)

    blocks = head_width // span

    def head_step(i):
        step = (i + 1) // 2

        @pl.when((lax.rem(i, 2) == 1) & (step <= last))
        def _():
            for b in range(PARTS):
                for way, whole in ways:
                    way(step - 1, b).wait_recv()
                    if whole(b):
                        way(step, b).start()
                    else:
                        pl.when(step < last)(lambda: way(step, b).start())

        slot = slot_of(i)
        head = lax.rem(z + slot, n_seq)

        def both(j):
            query_gradient(slot, head, j, *probabilities(slot, head, j))

        loop(0, blocks, both)
        store(0, i, head).start()
        store(1, i, head).start()

    loop(0, n_seq - 1, head_step)
    for b in range(PARTS):
        for way, whole in ways:
            if whole(b):
                way(last, b).wait_recv()
    far = n_seq // 2
    far_head = lax.rem(z + far, n_seq)

    def far_first(j):
        unused, prob, delta = probabilities(far, far_head, j)
        prob_buf[j] = prob
        delta_buf[j] = jnp.broadcast_to(delta, (block, LANES))

    def far_second(j):
        g = grad_rows(cols_of(far_head, j))
        query_gradient(far, far_head, j, g, prob_buf[j], delta_buf[j][:, :1])

    loop(0, blocks, far_first)
    store(0, n_seq - 1, far_head).start()

    def col_copy(k):
        target = lax.rem(z + k, n_seq)
        return remote(
            small.at[:, lanes_of(target)], col_in.at[k], col_ss.at[k], col_rs.at[k], (p, target)
        )

    loop(1, n_seq, lambda k: col_copy(k).start())
    loop(0, blocks, far_second)
    store(1, n_seq - 1, far_head).start()
    own = small[:, lanes_of(z)]
    for k in range(1, n_seq):
        col_copy(k).wait_recv()
        own = own + col_in[k]
    own = ADAPTER_SCALE * own
    for j in range(fit):
        moved = own[:rank]
        if j > 0:
            moved = pltpu.roll(moved, LANES - j * img_rows, 1)
        back_out[j] = moved.astype(jnp.bfloat16)
    wide = total.shape[1]
    pieces = 2 * (wide // LANES)
    total[:, width:] = jnp.zeros((rank, wide - width), jnp.float32)
    total[:, wide - LANES :] = own[rank:]

    def back_copy(n):
        j, s = lax.rem(n, fit), n // fit
        o = lax.rem(p + n_dp - fit * z - j, n_dp)
        return remote(back_out.at[j], back_in.at[p], back_ss.at[n], back_rs.at[p], (o, s))

    def unless_own(n, act):
        pl.when((n != 0) | (z != 0))(act)

    loop(0, fit * n_seq, lambda n: unless_own(n, lambda: back_copy(n).start()))

    @pl.when(z == 0)
    def _():
        back_in[p] = back_out[0]

    def back_wait(k):
        g = lax.rem(p + k, n_dp)
        copy = remote(
            back_out.at[0], back_in.at[g], back_ss.at[0], back_rs.at[g], (g, k // fit)
        )
        unless_own(k, lambda: copy.wait_recv())

    loop(0, n_dp, back_wait)

    lane_rank = lax.broadcasted_iota(jnp.int32, (rank, LANES), 1)
    pieces_in = []
    for first in range(0, img_dev, fit):
        piece = jnp.zeros((rank, LANES), jnp.float32)
        for i in range(fit):
            held = back_in[reader_ref[first + i]].astype(jnp.float32)
            if i > 0:
                held = pltpu.roll(held, i * img_rows, 1)
            piece = jnp.where(lane_rank // img_rows == i, held, piece)
        pieces_in.append(piece.astype(jnp.bfloat16))
    total[:, :width] = jnp.dot(
        jnp.concatenate(pieces_in, axis=1), tiles[...], preferred_element_type=jnp.float32
    )

    def piece_of(j):
        return total.at[
            pl.ds(pl.multiple_of(lax.rem(j, 2) * 8, 8), 8),
            lanes_of(j // 2),
        ]

    def sum_copy(j):
        k = lax.rem(j - p + n_dp, n_dp)
        return remote(piece_of(j), sum_in.at[k], sum_ss.at[j], sum_rs.at[k], (j, z))

    loop(0, pieces, lambda j: pl.when(j != p)(lambda: sum_copy(j).start()))

    def done_copy(k, j):
        g = lax.rem(p + k, n_dp)
        return remote(done.at[j], done.at[j], done_ss.at[k], done_rs.at[j], (g, z))

    @pl.when(p < pieces)
    def _():
        def take(k, acc):
            remote(
                piece_of(p), sum_in.at[k], sum_ss.at[0], sum_rs.at[k], (p, z)
            ).wait_recv()
            return acc + sum_in[k]

        done[p] = lax.fori_loop(1, n_dp, take, piece_of(p)[...])
        loop(1, n_dp, lambda k: done_copy(k, p).start())

    def ring_sent(t):
        for s in range(chunks):
            for copy in hop(t, s):
                copy.wait_send()

    loop(0, n_seq - 1, ring_sent)
    loop(1, n_seq, lambda k: up_copy(k, z).wait_send())
    loop(1, n_dp, lambda k: kv_copy(k).wait_send())
    loop(1, n_dp, lambda k: ext_copy(k).wait_send())
    for t in range(last + 1):
        for b in range(PARTS):
            for way, whole in ways:
                if t < last or whole(b):
                    way(t, b).wait_send()
    loop(1, n_seq, lambda k: col_copy(k).wait_send())
    loop(0, fit * n_seq, lambda n: unless_own(n, lambda: back_copy(n).wait_send()))
    loop(0, pieces, lambda j: pl.when(j != p)(lambda: sum_copy(j).wait_send()))

    def stored(i):
        head = lax.rem(z + slot_of(i), n_seq)
        store(0, i, head).wait()
        store(1, i, head).wait()

    loop(0, n_seq, stored)

    loop(0, pieces, lambda j: pl.when(j != p)(lambda: done_copy(0, j).wait_recv()))
    for j in range(pieces - 2):
        r, c = 8 * (j % 2), LANES * (j // 2)
        fill = min(LANES, width - c)
        if fill > 0:
            down_ref[r : r + 8, c : c + fill] = done[j][:, :fill]
    up_out_ref[:8, :] = done[pieces - 2]
    up_out_ref[8:, :] = done[pieces - 1]

    @pl.when(p < pieces)
    def _():
        loop(1, n_dp, lambda k: done_copy(k, p).wait_send())


def per_device(
    queries,
    output_gradient,
    tiles,
    frozen_key_weight,
    frozen_value_weight,
    key_norm_gain,
    adapter_down_weight,
    adapter_up_weight,
    gate,
    document_lengths,
    image_reader_group,
    image_document,
):
    n_dp, n_seq = lax.axis_size("dp"), lax.axis_size("seq")
    docs = document_lengths.shape[1]
    rank = adapter_up_weight.shape[0]
    img_dev, img_rows, width = tiles.shape
    rows = img_dev * img_rows
    tokens, columns = queries.shape
    keys = n_dp * img_rows
    block = min(HEADS_AT_ONCE * LANES, columns // n_seq) // LANES * tokens
    blocks = (columns // n_seq) // LANES * tokens // block
    wide = -(-width // LANES) * LANES + LANES
    pieces = 2 * (wide // LANES)
    fan = (LANES // img_rows) * n_seq
    chunks = rows // CHUNK
    any_space = pl.BlockSpec(memory_space=pl.ANY)
    vmem = pl.BlockSpec(memory_space=pltpu.VMEM)
    smem = pl.BlockSpec(memory_space=pltpu.SMEM)
    f32, bf16 = jnp.float32, jnp.bfloat16

    def held(*shape, kind=bf16):
        return pltpu.VMEM(shape, kind)

    dma = pltpu.SemaphoreType.DMA
    gated, query_grad, down_rows, up_grad = pl.pallas_call(
        functools.partial(fused_kernel, n_dp, n_seq, docs),
        out_shape=(
            jax.ShapeDtypeStruct((tokens, columns), bf16),
            jax.ShapeDtypeStruct((tokens, columns), bf16),
            jax.ShapeDtypeStruct((rank, width), f32),
            jax.ShapeDtypeStruct((rank, LANES), f32),
        ),
        in_specs=[any_space] * 6 + [vmem] * 2 + [smem] * 4,
        out_specs=(any_space, any_space, vmem, vmem),
        scratch_shapes=[
            held(tokens, columns),
            held(tokens, columns),
            held(tokens, columns),
            held(tokens, columns),
            held(rows, width),
            held(width, n_seq * LANES),
            held(width, n_seq * LANES),
            held(rank, width),
            held(rows, LANES, kind=f32),
            held(rows, LANES, kind=f32),
            held(n_seq, rows, LANES, kind=f32),
            held(n_seq, rows, LANES),
            held(rank, rows, kind=f32),
            held(rank, rows),
            held(n_seq, rank, rows),
            held(n_seq, rank, LANES),
            pltpu.SMEM((n_dp,), jnp.int32),
            pltpu.SMEM((n_dp,), jnp.int32),
            held(img_dev, img_rows, 2 * LANES),
            held(img_dev, img_rows, LANES),
            held(n_dp, img_rows, 2 * LANES),
            held(n_dp, img_rows, LANES),
            held(n_seq, keys, 2 * LANES),
            held(keys, LANES),
            held(block, LANES),
            held(blocks, block, keys, kind=f32),
            held(blocks, block, LANES, kind=f32),
            held(2 * rank, keys, kind=f32),
            held(n_seq, 2 * rank, LANES, kind=f32),
            held(LANES // img_rows, rank, LANES),
            held(n_dp, rank, LANES),
            held(rank, wide, kind=f32),
            held(n_dp, 8, LANES, kind=f32),
            held(pieces, 8, LANES, kind=f32),
            dma((6,)),
            dma((2, n_seq)),
            dma((n_seq, chunks)),
            dma((n_seq, chunks)),
            dma((n_seq, chunks)),
            dma((n_seq, chunks)),
            dma((n_seq,)),
            dma((n_seq,)),
            dma((n_seq,)),
            dma((n_seq,)),
            dma((n_dp,)),
            dma((n_dp,)),
            dma((n_dp,)),
            dma((n_dp,)),
            dma((2, n_seq // 2, PARTS)),
            dma((2, n_seq // 2, PARTS)),
            dma((n_seq,)),
            dma((n_seq,)),
            dma((fan,)),
            dma((n_dp,)),
            dma((pieces,)),
            dma((n_dp,)),
            dma((n_dp,)),
            dma((pieces,)),
        ],
        compiler_params=pltpu.CompilerParams(
            collective_id=0, has_side_effects=True, vmem_limit_bytes=58 << 20
        ),
    )(
        queries,
        output_gradient,
        tiles.reshape(rows, width),
        frozen_key_weight,
        frozen_value_weight,
        adapter_down_weight.T,
        adapter_up_weight,
        key_norm_gain.reshape(1, -1),
        gate,
        document_lengths,
        image_reader_group,
        image_document,
    )
    return (gated, query_grad, down_rows.T, up_grad)


def solution(mesh):
    placed = (
        P(("dp", "seq"), None),
        P(("dp", "seq"), None),
        P("dp", None, "seq"),
        P("seq", None),
        P("seq", None),
        P(),
        P("seq", None),
        P(None, "seq"),
        P(),
        P("dp", None),
        P("dp"),
        P("dp"),
    )
    return jax.shard_map(
        per_device,
        mesh=mesh,
        in_specs=placed,
        out_specs=(P(("dp", "seq"), None), P(("dp", "seq"), None), P("seq", None), P(None, "seq")),
        check_vma=False,
    )
```

time: 591 us -> 144 us (0.24); the launches traced: 581 us -> 144 us
  blocking collectives: 254 us -> 0 us
  Pallas kernels: 0 us -> 137 us
  waiting for transfers between devices: 90.5 us -> 0 us
  other arithmetic: 65.1 us -> 0 us
  matrix products: 57 us -> 0 us
  starting transfers between devices: 49 us -> 0 us
  local copies, waits for them, and re-layouts: 49.8 us -> 5.8 us
  between operations: 15.3 us -> 1.3 us
    psum x3 -> x0, blocking collectives: 254 us -> none  [the longest x1 126 us: per_device(): lax.psum(down_part.astype(jnp.bfloat16), 'dp').astype(jnp.float32)]
    pallas_call x0 -> x1, Pallas kernels: none -> 137 us  [per_device(): pl.pallas_call(functools.partial(fused_kernel, n_dp, n_seq, docs), out_sh...]
    all_to_all x7 -> x0, waiting for transfers between devices: 90.5 us -> none  [the longest x1 65.8 us: per_device(): lax.all_to_all(queries, 'seq', split_axis=1, concat_axis=0, tiled=True)]
    dot_general x18 -> x0, matrix products: 57 us -> none  [the longest x2 20.5 us: attend(): jnp.einsum('gnm,md->ngd', score_grad, key_rows[0], preferred_element_type...]
    all_to_all x7 -> x0, starting transfers between devices: 48.9 us -> none  [the longest x1 10.8 us: per_device(): lax.all_to_all(outgoing, 'dp', split_axis=0, concat_axis=0, tiled=True)]
    sub x2 -> x0, other arithmetic: 35.3 us -> none  [attend(): weights = jnp.exp(scores - row_max)]
    convert_element_type x7 -> x0, other arithmetic: 20.3 us -> none  [the longest x2 14 us: attend(): prob_bf16 = prob_f32.astype(jnp.bfloat16)]
    all_to_all x4 -> x0, local copies, waits for them, and re-layouts: 11.7 us -> none  [the longest x1 3.9 us: per_device(): lax.all_to_all(head_gated, 'seq', split_axis=0, concat_axis=1, tiled=True)]
  transfers between devices with their start and end apart: 8 -> 0, of which waited for: 3 -> 0; matrix products, arithmetic and copies ran while one was open for 14% -> 0% of each run, Pallas kernels for 0% -> 0%
where the time goes in v2:
time: 144 us
  Pallas kernels  137 us (95%)
  local copies, waits for them, and re-layouts  5.8 us (4%)
    pallas_call x1, Pallas kernels, per_device(): pl.pallas_call(functools.partial(fused_kernel, n_dp, n_seq, docs), out_sh...  137 us
    unnamed x10, local copies, waits for them, and re-layouts  5.8 us

profile of v2, /device:TPU:1, one launch (start us, length us, event | category | flops | bytes accessed | tf_op | source)
XLA Modules:
  0.0 143.7 jit_solution(15723740013491938042)
XLA Ops:
  1.3 136.6 %shard_map.147 = (bf16[128,8192]{1,0:T(8,128)(2,1)}, bf16[128,8192]{1,0:T(8,128)(2,1)}, f32[16,960]{1,0:T(8,128)}, f32[16,128]{1,0:T(8,128)}) custom-call(bf16[128,8192]{1,0:T(8,128)(2,1)} %query_hbm.1, bf16[128,8192]{1,0:T(8,128)(2,1)} %grad_hbm.1, bf16[512,960]{1,0:T(8,128)(2,1)} %bitcast.4, bf16[960,1024]{1,0:T(8,128)(2,1)} %wk_hbm.1, ...), custom_call_target="tpu_custom_call" | custom-call | tf_op jit(solution)/shard_map/pallas_call | solution.py:629
  137.8 0.0 copy-start
  137.9 3.2 %copy.21 = bf16[128,8192]{1,0:T(8,128)(2,1)} copy(bf16[128,8192]{1,0:T(8,128)(2,1)} %get-tuple-element.16) | data formatting | bytes 4194304
  141.1 0.0 copy-done
  141.1 0.0 copy-start.1
  141.1 0.0 copy-start.2
  141.1 1.3 copy.22
  142.4 0.0 copy-done.1
  142.4 0.6 copy.23
  143.1 0.0 copy-done.2
  143.1 0.6 copy.24
Async XLA Ops:
  137.8 3.3 %copy-start = (bf16[128,8192]{1,0:T(8,128)(2,1)S(1)}, bf16[128,8192]{1,0:T(8,128)(2,1)}, u32[]{:S(2)}) copy-start(bf16[128,8192]{1,0:T(8,128)(2,1)} %get-tuple-element.17) | copy-start | bytes 6291460
  141.1 1.3 copy-start.1
  141.1 2.0 %copy-start.2 = (f32[16,128]{1,0:T(8,128)S(1)}, f32[16,128]{1,0:T(8,128)}, u32[]{:S(2)}) copy-start(f32[16,128]{1,0:T(8,128)} %get-tuple-element.19) | copy-start | bytes 24580

commit v3 on v2

v3 whole, which is shorter than its diff:
```python
import functools

import jax
import jax.numpy as jnp
from jax import lax
from jax.experimental import pallas as pl
from jax.experimental.pallas import tpu as pltpu
from jax.sharding import PartitionSpec as P

EPS = 1e-05
ADAPTER_SCALE = 2.0
MASKED = -1e30
LANES = 128
CHUNK = 64
PARTS = 4
HEADS_AT_ONCE = 4
LAG = 2
LOG2_E = 1.4426950408889634
MESH = pl.DeviceIdType.MESH
NT = (((1,), (1,)), ((), ()))
TN = (((0,), (0,)), ((), ()))


def remote(src, dst, send_sem, recv_sem, target):
    return pltpu.make_async_remote_copy(
        src_ref=src,
        dst_ref=dst,
        send_sem=send_sem,
        recv_sem=recv_sem,
        device_id=target,
        device_id_type=MESH,
    )


def loop(first, last, body):
    def step(i, carry):
        body(i)
        return carry

    lax.fori_loop(first, last, step, 0)


def greet(barrier, target):
    pl.semaphore_signal(barrier, inc=1, device_id=target, device_id_type=MESH)


def fused_kernel(
    n_dp,
    n_seq,
    docs,
    query_hbm,
    grad_hbm,
    tiles_hbm,
    wk_hbm,
    wv_hbm,
    wd_hbm,
    up_hbm,
    gain_hbm,
    gate_hbm,
    length_hbm,
    reader_hbm,
    doc_hbm,
    gated_hbm,
    query_grad_hbm,
    down_hbm,
    up_out_hbm,
    query,
    grad,
    gated,
    query_grad,
    tiles,
    wk,
    wv,
    wd,
    up,
    gain,
    gate_s,
    lengths,
    reader,
    doc,
    own_k,
    own_v,
    sum_k,
    sum_v,
    low_own,
    low_out,
    low_in,
    up_all,
    pick,
    tag,
    rows_k,
    rows_v,
    ext_rows,
    k_out,
    v_out,
    ext_out,
    k_all,
    v_all,
    ext,
    ext_t,
    bias,
    probs,
    value_grad,
    small,
    col_in,
    back_out,
    back_in,
    total,
    sum_in,
    done,
    down_stage,
    up_stage,
    load_sem,
    store_sem,
    out_sem,
    k_ss,
    k_rs,
    v_ss,
    v_rs,
    low_ss,
    low_rs,
    up_ss,
    up_rs,
    route_ss,
    route_rs,
    ring_ss,
    ring_rs,
    col_ss,
    col_rs,
    back_ss,
    back_rs,
    sum_ss,
    sum_rs,
    done_ss,
    done_rs,
):
    p = lax.axis_index("dp")
    z = lax.axis_index("seq")
    rows, width = tiles.shape
    tokens, columns = query.shape
    rank = up.shape[0]
    img_dev, img_rows = rows_k.shape[:2]
    keys = ext.shape[0]
    head_width = columns // n_seq
    block = bias.shape[0]
    span = (block // tokens) * LANES
    blocks = head_width // span
    fit = LANES // img_rows
    half = rows // 2
    chunks = rows // CHUNK
    scale = LANES ** (-0.5)
    f32, bf16 = jnp.float32, jnp.bfloat16
    right = (p, lax.rem(z + 1, n_seq))
    left = (p, lax.rem(z + n_seq - 1, n_seq))

    def lanes_of(n, size=LANES):
        return pl.ds(pl.multiple_of(n * size, size), size)

    def load(n, source, into):
        return pltpu.make_async_copy(source, into, load_sem.at[n])

    load_tiles, load_wk = load(0, tiles_hbm, tiles), load(1, wk_hbm, wk)
    load_wv, load_wd = load(2, wv_hbm, wv), load(3, wd_hbm, wd)
    load_up, load_gain = load(4, up_hbm, up), load(5, gain_hbm, gain)
    load_gate, load_lengths = load(6, gate_hbm, gate_s), load(7, length_hbm, lengths)
    load_reader, load_doc = load(8, reader_hbm, reader), load(9, doc_hbm, doc)
    load_query, load_grad = load(10, query_hbm, query), load(11, grad_hbm, grad)
    for copy in (load_tiles, load_wk, load_wd, load_up, load_gain, load_gate, load_lengths):
        copy.start()
    for copy in (load_reader, load_doc, load_wv):
        copy.start()
    barrier = pltpu.get_barrier_semaphore()
    loop(1, n_seq, lambda k: greet(barrier, (p, lax.rem(z + k, n_seq))))
    loop(1, n_dp, lambda k: greet(barrier, (lax.rem(p + k, n_dp), z)))

    def greet_back(k):
        @pl.when((k != 0) | (z != 0))
        def _():
            greet(barrier, (lax.rem(p + k, n_dp), k // fit))

    loop(0, n_dp, greet_back)

    def own_part(t, weight, own):
        ahead = lax.rem(z + 2 * n_seq - 1 - t, n_seq)
        back = lax.rem(z + 1 + t, n_seq)
        for side, head in ((0, ahead), (1, back)):
            part = pl.ds(side * half, half)
            own[part, :] = jnp.dot(
                tiles[part, :], weight[:, lanes_of(head)], preferred_element_type=f32
            )

    order = [c + side * (chunks // 2) for c in range(chunks // 2) for side in (0, 1)]

    def hop(sums, ss, rs, t, s):
        target = right if s < chunks // 2 else left
        part = pl.ds(s * CHUNK, CHUNK)
        return remote(sums.at[t, part], sums.at[t + 1, part], ss.at[t, s], rs.at[t, s], target)

    def k_hop(t, s):
        return hop(sum_k, k_ss, k_rs, t, s)

    def v_hop(t, s):
        return hop(sum_v, v_ss, v_rs, t, s)

    def k_step(t):
        own_part(t, wk, own_k)
        for s in order:
            part = pl.ds(s * CHUNK, CHUNK)
            k_hop(t - 1, s).wait_recv()
            sum_k[t, part, :] = sum_k[t, part, :] + own_k[part, :]
            k_hop(t, s).start()

    def v_step(t):
        own_part(t, wv, own_v)
        for s in order:
            part = pl.ds(s * CHUNK, CHUNK)
            v_hop(t - 1, s).wait_recv()
            sum_v[t, part, :] = (sum_v[t, part, :].astype(f32) + own_v[part, :]).astype(bf16)
            v_hop(t, s).start()

    load_tiles.wait()
    load_wk.wait()
    own_part(0, wk, own_k)
    sum_k[0] = own_k[...]
    pl.semaphore_wait(barrier, n_seq - 1 + n_dp - 1 + n_dp - jnp.where(z == 0, 1, 0))
    for s in order:
        k_hop(0, s).start()

    def low_copy(k):
        target = (p, lax.rem(z + k, n_seq))
        return remote(low_out, low_in.at[k], low_ss.at[k], low_rs.at[k], target)

    def up_copy(k, slot):
        target = (p, lax.rem(z + k, n_seq))
        return remote(up, up_all.at[slot], up_ss.at[k], up_rs.at[k], target)

    load_wd.wait()
    load_up.wait()
    low_own[...] = lax.dot_general(wd[...], tiles[...], NT, preferred_element_type=f32)
    low_out[...] = low_own[...].astype(bf16)
    loop(1, n_seq, lambda k: low_copy(k).start())
    loop(1, n_seq, lambda k: up_copy(k, z).start())
    up_all[z] = up[...]
    load_query.start()
    load_grad.start()
    for copy in (load_gain, load_gate, load_lengths, load_reader, load_doc):
        copy.wait()

    def find(g):
        at, mark = jnp.int32(0), jnp.int32(docs)
        for i in range(img_dev):
            hit = reader[i] == g
            at = jnp.where(hit, i, at)
            mark = jnp.where(hit, doc[i], mark)
        pick[g] = at
        tag[g] = mark

    loop(0, n_dp, find)

    def route(n, out, into, k):
        g = lax.rem(p + k, n_dp)
        return remote(
            out.at[k],
            into.at[pl.ds(pl.multiple_of(k * img_rows, img_rows), img_rows)],
            route_ss.at[n, k],
            route_rs.at[n, k],
            (g, z),
        )

    def k_route(k):
        return route(0, k_out, k_all.at[0], k)

    def v_route(k):
        return route(1, v_out, v_all.at[0], k)

    def ext_route(k):
        return route(2, ext_out, ext, k)

    lane = lax.broadcasted_iota(jnp.int32, (img_rows, LANES), 1)

    def ext_block(g):
        mark = jnp.where(lane == rank + tag[g], 1.0, 0.0)
        low = ext_rows[pick[g]].astype(f32)
        return jnp.where(lane < rank, low, mark).astype(bf16)

    def send_ext(k):
        ext_out[k] = ext_block(lax.rem(p + k, n_dp))
        ext_route(k).start()

    def low_finish():
        loop(1, n_seq, lambda k: low_copy(k).wait_send())
        low_total = low_own[...]
        for k in range(1, n_seq):
            low_copy(k).wait_recv()
            low_total = low_total + low_in[k].astype(f32)
        low_rank = low_total.astype(bf16)
        low_out[...] = low_rank
        eye = lax.broadcasted_iota(jnp.int32, (rank, LANES), 0) == lax.broadcasted_iota(
            jnp.int32, (rank, LANES), 1
        )
        eye = jnp.where(eye, 1.0, 0.0).astype(bf16)
        low_rows = lax.dot_general(low_rank, eye, TN, preferred_element_type=f32)
        ext_rows[...] = low_rows.astype(bf16).reshape(img_dev, img_rows, LANES)

    lag = min(LAG, n_seq - 2)
    if lag > 0:
        loop(1, lag, k_step)
        k_step(lag)
    load_wv.wait()
    own_part(0, wv, own_v)
    sum_v[0] = own_v[...].astype(bf16)
    for s in order:
        v_hop(0, s).start()
    low_finish()
    both_steps = n_seq - 2 - lag
    each = -(-(n_dp - 1) // max(1, both_steps))

    def both_step(t):
        first = 1 + (t - lag - 1) * each
        loop(first, jnp.minimum(first + each, n_dp), send_ext)
        k_step(t)
        v_step(t - lag)

    loop(lag + 1, n_seq - 1, both_step)
    if both_steps == 0:
        loop(1, n_dp, send_ext)

    per_chunk = CHUNK // img_rows
    own_part(n_seq - 1, wk, own_k)
    for s in order:
        part = pl.ds(s * CHUNK, CHUNK)
        k_hop(n_seq - 2, s).wait_recv()
        key_raw = sum_k[n_seq - 1, part, :] + own_k[part, :]
        mean_square = jnp.mean(key_raw * key_raw, axis=-1, keepdims=True)
        key_rows = (key_raw * lax.rsqrt(mean_square + EPS) * gain[...]).astype(bf16)
        rows_k[pl.ds(s * per_chunk, per_chunk)] = key_rows.reshape(per_chunk, img_rows, LANES)

    def send_k(k):
        k_out[k] = rows_k[pick[lax.rem(p + k, n_dp)]]
        k_route(k).start()

    loop(1, n_dp, send_k)
    k_all[0, :img_rows, :] = rows_k[pick[p]]
    ext[:img_rows, :] = ext_block(p)

    loop(n_seq - 1 - lag, n_seq - 1, v_step)
    own_part(n_seq - 1, wv, own_v)
    low_up = lax.dot_general(low_out[...], up[...], TN, preferred_element_type=f32)
    own_v[...] = own_v[...] + ADAPTER_SCALE * low_up
    for s in order:
        part = pl.ds(s * CHUNK, CHUNK)
        v_hop(n_seq - 2, s).wait_recv()
        value = (sum_v[n_seq - 1, part, :].astype(f32) + own_v[part, :]).astype(bf16)
        rows_v[pl.ds(s * per_chunk, per_chunk)] = value.reshape(per_chunk, img_rows, LANES)

    last = n_seq // 2 - 1
    part_rows = keys // PARTS
    slots = n_dp // PARTS

    def gather(held, n):
        def ahead(t, b):
            part = pl.ds(pl.multiple_of(b * part_rows, part_rows), part_rows)
            source, into = lax.rem(n_seq - t, n_seq), n_seq - 1 - t
            return remote(
                held.at[source, part],
                held.at[into, part],
                ring_ss.at[n, t, b],
                ring_rs.at[n, t, b],
                right,
            )

        def back(t, b):
            part = pl.ds(pl.multiple_of(b * part_rows, part_rows), part_rows)
            return remote(
                held.at[t, part],
                held.at[t + 1, part],
                ring_ss.at[n + 1, t, b],
                ring_rs.at[n + 1, t, b],
                left,
            )

        return ((ahead, lambda b: b < PARTS // 2), (back, lambda b: b >= PARTS // 2))

    k_ways, v_ways = gather(k_all, 0), gather(v_all, 2)

    def gather_start(ways, arrived):
        for b in range(PARTS):
            loop(max(1, b * slots), (b + 1) * slots, lambda k: arrived(k).wait_recv())
            for way, whole in ways:
                if last > 0 or whole(b):
                    way(0, b).start()

    def forward(ways, t, b):
        for way, whole in ways:

            @pl.when((t <= last) | whole(b))
            def _():
                way(t - 1, b).wait_recv()

            @pl.when((t < last) | ((t == last) & whole(b)))
            def _():
                way(t, b).start()

    def after_block(ways, m):
        i = m // blocks
        step = (i + 1) // 2
        q = m - blocks * (2 * step - 1)
        per = PARTS // (2 * blocks)

        @pl.when(m == blocks - 1)
        def _():
            loop(0, PARTS, lambda b: forward(ways, 1, b))

        @pl.when((i >= 1) & (i < n_seq - 1))
        def _():
            loop(q * per, (q + 1) * per, lambda b: forward(ways, step + 1, b))

    def gather_sent(ways):
        for t in range(last + 1):
            for b in range(PARTS):
                for way, whole in ways:
                    if t < last or whole(b):
                        way(t, b).wait_send()

    gather_start(k_ways, k_route)

    def send_v(k):
        v_out[k] = rows_v[pick[lax.rem(p + k, n_dp)]]
        v_route(k).start()

    loop(1, n_dp, send_v)
    v_all[0, :img_rows, :] = rows_v[pick[p]]

    lane_tok = lax.broadcasted_iota(jnp.int32, (tokens, LANES), 1)
    place = lax.broadcasted_iota(jnp.int32, (tokens, LANES), 0) + z * tokens
    own_doc = jnp.zeros((tokens, LANES), jnp.int32)
    end = jnp.int32(0)
    for d in range(docs - 1):
        end = end + lengths[0, d]
        own_doc = own_doc + jnp.where(place >= end, 1, 0)
    other = (lane_tok >= rank) & (lane_tok <= rank + docs) & (lane_tok != rank + own_doc)
    penalty = jnp.where(other, MASKED, 0.0).astype(bf16)
    for n in range(block // tokens):
        bias[n * tokens : (n + 1) * tokens, :] = penalty
    small[...] = jnp.zeros_like(small)
    gate = jnp.tanh(jnp.full((1, LANES), gate_s[0], f32))
    loop(1, n_seq, lambda k: up_copy(k, lax.rem(z + n_seq - k, n_seq)).wait_recv())
    loop(1, n_dp, lambda k: ext_route(k).wait_recv())
    ext_t[...] = ext[...].T
    load_query.wait()
    load_grad.wait()

    def stack(ref, cols):
        part = ref[:, cols]
        return jnp.concatenate(
            [part[:, n * LANES : (n + 1) * LANES] for n in range(block // tokens)], axis=0
        )

    def unstack(x):
        return jnp.concatenate(
            [x[n * tokens : (n + 1) * tokens] for n in range(block // tokens)], axis=1
        )

    def where_is(m):
        i, j = m // blocks, lax.rem(m, blocks)
        slot = jnp.where(lax.rem(i, 2) == 1, n_seq - (i + 1) // 2, i // 2)
        head = lax.rem(z + slot, n_seq)
        cols = pl.ds(pl.multiple_of(head * head_width + j * span, span), span)
        return i, j, slot, head, cols

    def first_half(m):
        i, j, slot, head, cols = where_is(m)
        g = (gate * stack(grad, cols).astype(f32)).astype(bf16)
        grad[:, cols] = unstack(g)
        q = jnp.concatenate([stack(query, cols), bias[...]], axis=1)
        key_ext = jnp.concatenate([k_all[slot], ext[...]], axis=1)
        scores = lax.dot_general(q, key_ext, NT, preferred_element_type=f32)
        row_max = jnp.max(scores, axis=1, keepdims=True)
        weights = jnp.exp2((scores - row_max) * (scale * LOG2_E))
        prob = weights * (1.0 / jnp.sum(weights, axis=1, keepdims=True))
        prob = prob.astype(bf16)
        probs[i, pl.ds(pl.multiple_of(j * block, block), block), :] = prob
        part = lax.dot_general(g, prob, TN, preferred_element_type=f32)

        @pl.when(j == 0)
        def _():
            value_grad[...] = part

        @pl.when(j > 0)
        def _():
            value_grad[...] += part

        @pl.when(j == blocks - 1)
        def _():
            whole = value_grad[...].astype(bf16)
            small[:rank, :] += jnp.dot(up_all[head], whole, preferred_element_type=f32)
            small[rank:, lanes_of(head)] = lax.dot_general(
                ext_t[:rank, :], whole, NT, preferred_element_type=f32
            )

        @pl.when(m == max(blocks * (2 * last - 1), blocks) - 1)
        def _():
            gather_start(v_ways, v_route)

        after_block(k_ways, m)

    loop(0, n_seq * blocks, first_half)

    def col_copy(k):
        target = lax.rem(z + k, n_seq)
        return remote(
            small.at[:, lanes_of(target)], col_in.at[k], col_ss.at[k], col_rs.at[k], (p, target)
        )

    wide = total.shape[1]
    pieces = 2 * (wide // LANES)

    def back_copy(n):
        j, s = lax.rem(n, fit), n // fit
        o = lax.rem(p + n_dp - fit * z - j, n_dp)
        return remote(back_out.at[j], back_in.at[p], back_ss.at[n], back_rs.at[p], (o, s))

    def unless_own(n, act):
        pl.when((n != 0) | (z != 0))(act)

    def piece_of(j):
        return total.at[
            pl.ds(pl.multiple_of(lax.rem(j, 2) * 8, 8), 8),
            lanes_of(j // 2),
        ]

    def sum_copy(j):
        k = lax.rem(j - p + n_dp, n_dp)
        return remote(piece_of(j), sum_in.at[k], sum_ss.at[j], sum_rs.at[k], (j, z))

    def done_copy(k, j):
        g = lax.rem(p + k, n_dp)
        return remote(done.at[j], done.at[j], done_ss.at[k], done_rs.at[j], (g, z))

    def adapter_back():
        own = small[:, lanes_of(z)]
        for k in range(1, n_seq):
            col_copy(k).wait_recv()
            own = own + col_in[k]
        own = ADAPTER_SCALE * own
        for j in range(fit):
            moved = own[:rank]
            if j > 0:
                moved = pltpu.roll(moved, LANES - j * img_rows, 1)
            back_out[j] = moved.astype(bf16)
        total[:, width:] = jnp.zeros((rank, wide - width), f32)
        total[:, wide - LANES :] = own[rank:]
        loop(0, fit * n_seq, lambda n: unless_own(n, lambda: back_copy(n).start()))

        @pl.when(z == 0)
        def _():
            back_in[p] = back_out[0]

    def adapter_sum():
        def back_wait(k):
            g = lax.rem(p + k, n_dp)
            copy = remote(
                back_out.at[0], back_in.at[g], back_ss.at[0], back_rs.at[g], (g, k // fit)
            )
            unless_own(k, lambda: copy.wait_recv())

        loop(0, n_dp, back_wait)
        lane_rank = lax.broadcasted_iota(jnp.int32, (rank, LANES), 1)
        pieces_in = []
        for first in range(0, img_dev, fit):
            piece = jnp.zeros((rank, LANES), f32)
            for i in range(fit):
                held = back_in[reader[first + i]].astype(f32)
                if i > 0:
                    held = pltpu.roll(held, i * img_rows, 1)
                piece = jnp.where(lane_rank // img_rows == i, held, piece)
            pieces_in.append(piece.astype(bf16))
        total[:, :width] = jnp.dot(
            jnp.concatenate(pieces_in, axis=1), tiles[...], preferred_element_type=f32
        )
        loop(0, pieces, lambda j: pl.when(j != p)(lambda: sum_copy(j).start()))

    def adapter_done():
        @pl.when(p < pieces)
        def _():
            def take(k, acc):
                remote(
                    piece_of(p), sum_in.at[k], sum_ss.at[0], sum_rs.at[k], (p, z)
                ).wait_recv()
                return acc + sum_in[k]

            done[p] = lax.fori_loop(1, n_dp, take, piece_of(p)[...])
            loop(1, n_dp, lambda k: done_copy(k, p).start())

    loop(1, n_seq, lambda k: col_copy(k).start())

    def store(n, i, head):
        cols = lanes_of(head, head_width)
        source, into = ((gated, gated_hbm), (query_grad, query_grad_hbm))[n]
        return pltpu.make_async_copy(source.at[:, cols], into.at[:, cols], store_sem.at[n, i])

    end_block = n_seq * blocks - 1

    def second_half(m):
        i, j, slot, head, cols = where_is(m)
        g = stack(grad, cols)
        prob = probs[i, pl.ds(pl.multiple_of(j * block, block), block), :]
        value = v_all[slot]
        attended = jnp.dot(prob, value, preferred_element_type=f32)
        prob_grad = lax.dot_general(g, value, NT, preferred_element_type=f32)
        gated[:, cols] = unstack((gate * attended).astype(bf16))
        delta = jnp.sum(g.astype(f32) * attended, axis=1, keepdims=True)
        score_grad = (prob.astype(f32) * (prob_grad - delta)).astype(bf16)
        out_grad = jnp.dot(score_grad, k_all[slot], preferred_element_type=f32)
        query_grad[:, cols] = unstack((out_grad * scale).astype(bf16))

        @pl.when(j == blocks - 1)
        def _():
            store(0, i, head).start()
            store(1, i, head).start()

        after_block(v_ways, m)
        pl.when(m == blocks - 1)(adapter_back)
        pl.when(m == min(3 * blocks - 1, end_block))(adapter_sum)
        pl.when(m == min(5 * blocks - 1, end_block))(adapter_done)

    loop(0, n_seq * blocks, second_half)

    loop(0, pieces, lambda j: pl.when(j != p)(lambda: done_copy(0, j).wait_recv()))
    for j in range(pieces - 2):
        r, c = 8 * (j % 2), LANES * (j // 2)
        fill = min(LANES, width - c)
        if fill > 0:
            down_stage[r : r + 8, c : c + fill] = done[j][:, :fill]
    up_stage[:8, :] = done[pieces - 2]
    up_stage[8:, :] = done[pieces - 1]
    store_down = pltpu.make_async_copy(down_stage, down_hbm, out_sem.at[0])
    store_up = pltpu.make_async_copy(up_stage, up_out_hbm, out_sem.at[1])
    store_down.start()
    store_up.start()

    def ring_sent(t):
        for s in range(chunks):
            k_hop(t, s).wait_send()
            v_hop(t, s).wait_send()

    loop(0, n_seq - 1, ring_sent)
    loop(1, n_seq, lambda k: up_copy(k, z).wait_send())
    for routed in (k_route, v_route, ext_route):
        loop(1, n_dp, lambda k: routed(k).wait_send())
    gather_sent(k_ways)
    gather_sent(v_ways)
    loop(1, n_seq, lambda k: col_copy(k).wait_send())
    loop(0, fit * n_seq, lambda n: unless_own(n, lambda: back_copy(n).wait_send()))
    loop(0, pieces, lambda j: pl.when(j != p)(lambda: sum_copy(j).wait_send()))

    @pl.when(p < pieces)
    def _():
        loop(1, n_dp, lambda k: done_copy(k, p).wait_send())

    def stored(m):
        i, j, slot, head, cols = where_is(m * blocks)
        store(0, i, head).wait()
        store(1, i, head).wait()

    loop(0, n_seq, stored)
    store_down.wait()
    store_up.wait()


def per_device(
    queries,
    output_gradient,
    tiles,
    frozen_key_weight,
    frozen_value_weight,
    key_norm_gain,
    adapter_down_weight,
    adapter_up_weight,
    gate,
    document_lengths,
    image_reader_group,
    image_document,
):
    n_dp, n_seq = lax.axis_size("dp"), lax.axis_size("seq")
    docs = document_lengths.shape[1]
    rank = adapter_up_weight.shape[0]
    img_dev, img_rows, width = tiles.shape
    rows = img_dev * img_rows
    tokens, columns = queries.shape
    keys = n_dp * img_rows
    block = min(HEADS_AT_ONCE * LANES, columns // n_seq) // LANES * tokens
    wide = -(-width // LANES) * LANES + LANES
    pieces = 2 * (wide // LANES)
    fit = LANES // img_rows
    fan = fit * n_seq
    chunks = rows // CHUNK
    any_space = pl.BlockSpec(memory_space=pl.ANY)
    f32, bf16 = jnp.float32, jnp.bfloat16

    def held(*shape, kind=bf16):
        return pltpu.VMEM(shape, kind)

    dma = pltpu.SemaphoreType.DMA
    gated, query_grad, down_rows, up_grad = pl.pallas_call(
        functools.partial(fused_kernel, n_dp, n_seq, docs),
        out_shape=(
            jax.ShapeDtypeStruct((tokens, columns), bf16),
            jax.ShapeDtypeStruct((tokens, columns), bf16),
            jax.ShapeDtypeStruct((rank, width), f32),
            jax.ShapeDtypeStruct((rank, LANES), f32),
        ),
        in_specs=[any_space] * 12,
        out_specs=(any_space,) * 4,
        scratch_shapes=[
            held(tokens, columns),
            held(tokens, columns),
            held(tokens, columns),
            held(tokens, columns),
            held(rows, width),
            held(width, n_seq * LANES),
            held(width, n_seq * LANES),
            held(rank, width),
            held(rank, LANES),
            held(1, LANES, kind=f32),
            pltpu.SMEM((1,), f32),
            pltpu.SMEM((1, docs), jnp.int32),
            pltpu.SMEM((img_dev,), jnp.int32),
            pltpu.SMEM((img_dev,), jnp.int32),
            held(rows, LANES, kind=f32),
            held(rows, LANES, kind=f32),
            held(n_seq, rows, LANES, kind=f32),
            held(n_seq, rows, LANES),
            held(rank, rows, kind=f32),
            held(rank, rows),
            held(n_seq, rank, rows),
            held(n_seq, rank, LANES),
            pltpu.SMEM((n_dp,), jnp.int32),
            pltpu.SMEM((n_dp,), jnp.int32),
            held(img_dev, img_rows, LANES),
            held(img_dev, img_rows, LANES),
            held(img_dev, img_rows, LANES),
            held(n_dp, img_rows, LANES),
            held(n_dp, img_rows, LANES),
            held(n_dp, img_rows, LANES),
            held(n_seq, keys, LANES),
            held(n_seq, keys, LANES),
            held(keys, LANES),
            held(LANES, keys),
            held(block, LANES),
            held(n_seq, columns // n_seq // LANES * tokens, keys),
            held(LANES, keys, kind=f32),
            held(2 * rank, keys, kind=f32),
            held(n_seq, 2 * rank, LANES, kind=f32),
            held(fit, rank, LANES),
            held(n_dp, rank, LANES),
            held(rank, wide, kind=f32),
            held(n_dp, 8, LANES, kind=f32),
            held(pieces, 8, LANES, kind=f32),
            held(rank, width, kind=f32),
            held(rank, LANES, kind=f32),
            dma((12,)),
            dma((2, n_seq)),
            dma((2,)),
            dma((n_seq, chunks)),
            dma((n_seq, chunks)),
            dma((n_seq, chunks)),
            dma((n_seq, chunks)),
            dma((n_seq,)),
            dma((n_seq,)),
            dma((n_seq,)),
            dma((n_seq,)),
            dma((3, n_dp)),
            dma((3, n_dp)),
            dma((4, n_seq // 2, PARTS)),
            dma((4, n_seq // 2, PARTS)),
            dma((n_seq,)),
            dma((n_seq,)),
            dma((fan,)),
            dma((n_dp,)),
            dma((pieces,)),
            dma((n_dp,)),
            dma((n_dp,)),
            dma((pieces,)),
        ],
        compiler_params=pltpu.CompilerParams(
            collective_id=0, has_side_effects=True, vmem_limit_bytes=58 << 20
        ),
    )(
        queries,
        output_gradient,
        tiles.reshape(rows, width),
        frozen_key_weight,
        frozen_value_weight,
        adapter_down_weight.T,
        adapter_up_weight,
        key_norm_gain.reshape(1, -1),
        gate,
        document_lengths,
        image_reader_group,
        image_document,
    )
    return (gated, query_grad, down_rows.T, up_grad)


def solution(mesh):
    placed = (
        P(("dp", "seq"), None),
        P(("dp", "seq"), None),
        P("dp", None, "seq"),
        P("seq", None),
        P("seq", None),
        P(),
        P("seq", None),
        P(None, "seq"),
        P(),
        P("dp", None),
        P("dp"),
        P("dp"),
    )
    return jax.shard_map(
        per_device,
        mesh=mesh,
        in_specs=placed,
        out_specs=(P(("dp", "seq"), None), P(("dp", "seq"), None), P("seq", None), P(None, "seq")),
        check_vma=False,
    )
```

time: 144 us -> 128 us (0.89)
  Pallas kernels: 137 us -> 121 us
    pallas_call x1, Pallas kernels: 137 us -> 121 us  [per_device(): pl.pallas_call(functools.partial(fused_kernel, n_dp, n_seq, docs), out_sh...]
where the time goes in v3:
time: 128 us
  Pallas kernels  121 us (95%)
  local copies, waits for them, and re-layouts  5.8 us (5%)
  between operations  1.3 us (1%)
    pallas_call x1, Pallas kernels, per_device(): pl.pallas_call(functools.partial(fused_kernel, n_dp, n_seq, docs), out_sh...  121 us
    unnamed x10, local copies, waits for them, and re-layouts  5.8 us

profile of v3, /device:TPU:1, one launch (start us, length us, event | category | flops | bytes accessed | tf_op | source)
XLA Modules:
  0.0 128.0 jit_solution(11455741572761356897)
XLA Ops:
  1.3 120.9 %shard_map.147 = (bf16[128,8192]{1,0:T(8,128)(2,1)}, bf16[128,8192]{1,0:T(8,128)(2,1)}, f32[16,960]{1,0:T(8,128)}, f32[16,128]{1,0:T(8,128)}) custom-call(bf16[128,8192]{1,0:T(8,128)(2,1)} %query_hbm.1, bf16[128,8192]{1,0:T(8,128)(2,1)} %grad_hbm.1, bf16[512,960]{1,0:T(8,128)(2,1)} %bitcast.4, bf16[960,1024]{1,0:T(8,128)(2,1)} %wk_hbm.1, ...), custom_call_target="tpu_custom_call" | custom-call | tf_op jit(solution)/shard_map/pallas_call | solution.py:705
  122.2 0.0 copy-start
  122.2 3.2 %copy.21 = bf16[128,8192]{1,0:T(8,128)(2,1)} copy(bf16[128,8192]{1,0:T(8,128)(2,1)} %get-tuple-element.16) | data formatting | bytes 4194304
  125.5 0.0 copy-done
  125.5 0.0 copy-start.1
  125.5 0.0 copy-start.2
  125.5 1.3 %copy.22 = bf16[128,8192]{1,0:T(8,128)(2,1)} copy(bf16[128,8192]{1,0:T(8,128)(2,1)S(1)} %copy-done) | data formatting | bytes 4194304
  126.8 0.0 copy-done.1
  126.8 0.6 copy.23
  127.4 0.0 copy-done.2
  127.4 0.6 copy.24
Async XLA Ops:
  122.2 3.3 %copy-start = (bf16[128,8192]{1,0:T(8,128)(2,1)S(1)}, bf16[128,8192]{1,0:T(8,128)(2,1)}, u32[]{:S(2)}) copy-start(bf16[128,8192]{1,0:T(8,128)(2,1)} %get-tuple-element.17) | copy-start | bytes 6291460
  125.5 1.3 %copy-start.1 = (f32[16,960]{1,0:T(8,128)S(1)}, f32[16,960]{1,0:T(8,128)}, u32[]{:S(2)}) copy-start(f32[16,960]{1,0:T(8,128)} %get-tuple-element.10) | copy-start | bytes 184324
  125.5 2.0 %copy-start.2 = (f32[16,128]{1,0:T(8,128)S(1)}, f32[16,128]{1,0:T(8,128)}, u32[]{:S(2)}) copy-start(f32[16,128]{1,0:T(8,128)} %get-tuple-element.19) | copy-start | bytes 24580

commit v4 on v3

--- a/solution.py
+++ b/solution.py
@@ -11,10 +11,8 @@
 ADAPTER_SCALE = 2.0
 MASKED = -1e30
 LANES = 128
-CHUNK = 64
 PARTS = 4
 HEADS_AT_ONCE = 4
-LAG = 2
 LOG2_E = 1.4426950408889634
 MESH = pl.DeviceIdType.MESH
 NT = (((1,), (1,)), ((), ()))
@@ -78,8 +76,7 @@
     lengths,
     reader,
     doc,
-    own_k,
-    own_v,
+    own,
     sum_k,
     sum_v,
     low_own,
@@ -112,27 +109,12 @@
     up_stage,
     load_sem,
     store_sem,
-    out_sem,
-    k_ss,
-    k_rs,
-    v_ss,
-    v_rs,
-    low_ss,
-    low_rs,
-    up_ss,
-    up_rs,
-    route_ss,
-    route_rs,
-    ring_ss,
-    ring_rs,
-    col_ss,
-    col_rs,
-    back_ss,
-    back_rs,
-    sum_ss,
-    sum_rs,
-    done_ss,
-    done_rs,
+    sent_sem,
+    all_sem,
+    sum_sem,
+    route_sem,
+    ring_sem,
+    done_sem,
 ):
     p = lax.axis_index("dp")
     z = lax.axis_index("seq")
@@ -147,7 +129,8 @@
     blocks = head_width // span
     fit = LANES // img_rows
     half = rows // 2
-    chunks = rows // CHUNK
+    mid = n_seq // 2
+    sum_rows = rows // PARTS
     scale = LANES ** (-0.5)
     f32, bf16 = jnp.float32, jnp.bfloat16
     right = (p, lax.rem(z + 1, n_seq))
@@ -180,67 +163,91 @@
 
     loop(0, n_dp, greet_back)
 
-    def own_part(t, weight, own):
-        ahead = lax.rem(z + 2 * n_seq - 1 - t, n_seq)
-        back = lax.rem(z + 1 + t, n_seq)
-        for side, head in ((0, ahead), (1, back)):
-            part = pl.ds(side * half, half)
-            own[part, :] = jnp.dot(
-                tiles[part, :], weight[:, lanes_of(head)], preferred_element_type=f32
-            )
-
-    order = [c + side * (chunks // 2) for c in range(chunks // 2) for side in (0, 1)]
-
-    def hop(sums, ss, rs, t, s):
-        target = right if s < chunks // 2 else left
-        part = pl.ds(s * CHUNK, CHUNK)
-        return remote(sums.at[t, part], sums.at[t + 1, part], ss.at[t, s], rs.at[t, s], target)
-
-    def k_hop(t, s):
-        return hop(sum_k, k_ss, k_rs, t, s)
-
-    def v_hop(t, s):
-        return hop(sum_v, v_ss, v_rs, t, s)
-
-    def k_step(t):
-        own_part(t, wk, own_k)
-        for s in order:
-            part = pl.ds(s * CHUNK, CHUNK)
-            k_hop(t - 1, s).wait_recv()
-            sum_k[t, part, :] = sum_k[t, part, :] + own_k[part, :]
-            k_hop(t, s).start()
-
-    def v_step(t):
-        own_part(t, wv, own_v)
-        for s in order:
-            part = pl.ds(s * CHUNK, CHUNK)
-            v_hop(t - 1, s).wait_recv()
-            sum_v[t, part, :] = (sum_v[t, part, :].astype(f32) + own_v[part, :]).astype(bf16)
-            v_hop(t, s).start()
+    def all_sent(n, region):
+        remote(region, region, sent_sem.at[n], all_sem.at[0], right).wait_send()
+
+    def all_here(region, sem):
+        remote(region, region, sent_sem.at[0], sem, right).wait_recv()
+
+    def in_part(b):
+        return pl.ds(b * sum_rows, sum_rows)
+
+    def goes(side, b):
+        return (b < PARTS // 2) == (side == 0)
+
+    def hop(n, side, t, b):
+        sums = (sum_k, sum_v)[n]
+        at = side * (mid + 1) + t
+        return remote(
+            sums.at[at, in_part(b)],
+            sums.at[at + 1, in_part(b)],
+            sent_sem.at[n],
+            sum_sem.at[n, side, t, b],
+            (right, left)[side],
+        )
+
+    def own_part(n, head):
+        weight = (wk, wv)[n]
+        return jnp.dot(tiles[...], weight[:, lanes_of(head)], preferred_element_type=f32)
+
+    def first_sums(n):
+        sums = (sum_k, sum_v)[n]
+        part = own_part(n, lax.rem(z + mid, n_seq)).astype(sums.dtype)
+        sums[0, :half, :] = part[:half]
+        sums[mid + 1, half:, :] = part[half:]
+
+    def first_sends(n):
+        for b in range(PARTS):
+            hop(n, 0 if goes(0, b) else 1, 0, b).start()
+
+    def sum_step(n, t):
+        sums = (sum_k, sum_v)[n]
+        own[0] = own_part(n, lax.rem(z + mid - t, n_seq))
+        own[1] = own_part(n, lax.rem(z + mid + t, n_seq))
+        for c in range(PARTS):
+            for side in (0, 1):
+                b = c if side == 0 else (c + PARTS // 2) % PARTS
+                at = side * (mid + 1) + t
+                total_here = own[side, in_part(b), :]
+                if t > 1 or goes(side, b):
+                    hop(n, side, t - 1, b).wait_recv()
+                    total_here = total_here + sums[at, in_part(b), :].astype(f32)
+                sums[at, in_part(b), :] = total_here.astype(sums.dtype)
+                hop(n, side, t, b).start()
+
+    def last_sums(n, b):
+        sums = (sum_k, sum_v)[n]
+        total_here = own[0, in_part(b), :]
+        for side in (0, 1):
+            if mid > 1 or goes(side, b):
+                hop(n, side, mid - 1, b).wait_recv()
+                at = side * (mid + 1) + mid
+                total_here = total_here + sums[at, in_part(b), :].astype(f32)
+        return total_here
 
     load_tiles.wait()
     load_wk.wait()
-    own_part(0, wk, own_k)
-    sum_k[0] = own_k[...]
+    first_sums(0)
     pl.semaphore_wait(barrier, n_seq - 1 + n_dp - 1 + n_dp - jnp.where(z == 0, 1, 0))
-    for s in order:
-        k_hop(0, s).start()
+    first_sends(0)
 
     def low_copy(k):
         target = (p, lax.rem(z + k, n_seq))
-        return remote(low_out, low_in.at[k], low_ss.at[k], low_rs.at[k], target)
-
-    def up_copy(k, slot):
+        return remote(low_out, low_in.at[k], sent_sem.at[2], all_sem.at[1], target)
+
+    def up_copy(k):
         target = (p, lax.rem(z + k, n_seq))
-        return remote(up, up_all.at[slot], up_ss.at[k], up_rs.at[k], target)
+        return remote(up, up_all.at[k], sent_sem.at[3], all_sem.at[2], target)
+
+    others = pl.ds(1, n_seq - 1)
 
     load_wd.wait()
     load_up.wait()
     low_own[...] = lax.dot_general(wd[...], tiles[...], NT, preferred_element_type=f32)
     low_out[...] = low_own[...].astype(bf16)
     loop(1, n_seq, lambda k: low_copy(k).start())
-    loop(1, n_seq, lambda k: up_copy(k, z).start())
-    up_all[z] = up[...]
+    loop(1, n_seq, lambda k: up_copy(k).start())
+    up_all[0] = up[...]
     load_query.start()
     load_grad.start()
     for copy in (load_gain, load_gate, load_lengths, load_reader, load_doc):
@@ -257,13 +264,21 @@
 
     loop(0, n_dp, find)
 
+    part_rows = keys // PARTS
+    slots = n_dp // PARTS
+
+    def routed(n, into, b):
+        skip = img_rows if b == 0 else 0
+        part = into.at[pl.ds(b * part_rows + skip, part_rows - skip)]
+        all_here(part, route_sem.at[n, b])
+
     def route(n, out, into, k):
         g = lax.rem(p + k, n_dp)
         return remote(
             out.at[k],
             into.at[pl.ds(pl.multiple_of(k * img_rows, img_rows), img_rows)],
-            route_ss.at[n, k],
-            route_rs.at[n, k],
+            sent_sem.at[4 + n],
+            route_sem.at[n, k // slots],
             (g, z),
         )
 
@@ -288,10 +303,10 @@
         ext_route(k).start()
 
     def low_finish():
-        loop(1, n_seq, lambda k: low_copy(k).wait_send())
+        all_sent(2, low_in.at[others])
+        all_here(low_in.at[others], all_sem.at[1])
         low_total = low_own[...]
         for k in range(1, n_seq):
-            low_copy(k).wait_recv()
             low_total = low_total + low_in[k].astype(f32)
         low_rank = low_total.astype(bf16)
         low_out[...] = low_rank
@@ -302,38 +317,25 @@
         low_rows = lax.dot_general(low_rank, eye, TN, preferred_element_type=f32)
         ext_rows[...] = low_rows.astype(bf16).reshape(img_dev, img_rows, LANES)
 
-    lag = min(LAG, n_seq - 2)
-    if lag > 0:
-        loop(1, lag, k_step)
-        k_step(lag)
+    for t in range(1, mid):
+        if t == mid - 1:
+            low_finish()
+            loop(1, n_dp, send_ext)
+        sum_step(0, t)
+    if mid == 1:
+        low_finish()
+        loop(1, n_dp, send_ext)
     load_wv.wait()
-    own_part(0, wv, own_v)
-    sum_v[0] = own_v[...].astype(bf16)
-    for s in order:
-        v_hop(0, s).start()
-    low_finish()
-    both_steps = n_seq - 2 - lag
-    each = -(-(n_dp - 1) // max(1, both_steps))
-
-    def both_step(t):
-        first = 1 + (t - lag - 1) * each
-        loop(first, jnp.minimum(first + each, n_dp), send_ext)
-        k_step(t)
-        v_step(t - lag)
-
-    loop(lag + 1, n_seq - 1, both_step)
-    if both_steps == 0:
-        loop(1, n_dp, send_ext)
-
-    per_chunk = CHUNK // img_rows
-    own_part(n_seq - 1, wk, own_k)
-    for s in order:
-        part = pl.ds(s * CHUNK, CHUNK)
-        k_hop(n_seq - 2, s).wait_recv()
-        key_raw = sum_k[n_seq - 1, part, :] + own_k[part, :]
+    first_sums(1)
+    first_sends(1)
+
+    per_part = sum_rows // img_rows
+    own[0] = own_part(0, z)
+    for b in range(PARTS):
+        key_raw = last_sums(0, b)
         mean_square = jnp.mean(key_raw * key_raw, axis=-1, keepdims=True)
         key_rows = (key_raw * lax.rsqrt(mean_square + EPS) * gain[...]).astype(bf16)
-        rows_k[pl.ds(s * per_chunk, per_chunk)] = key_rows.reshape(per_chunk, img_rows, LANES)
+        rows_k[pl.ds(b * per_part, per_part)] = key_rows.reshape(per_part, img_rows, LANES)
 
     def send_k(k):
         k_out[k] = rows_k[pick[lax.rem(p + k, n_dp)]]
@@ -343,19 +345,15 @@
     k_all[0, :img_rows, :] = rows_k[pick[p]]
     ext[:img_rows, :] = ext_block(p)
 
-    loop(n_seq - 1 - lag, n_seq - 1, v_step)
-    own_part(n_seq - 1, wv, own_v)
+    for t in range(1, mid):
+        sum_step(1, t)
     low_up = lax.dot_general(low_out[...], up[...], TN, preferred_element_type=f32)
-    own_v[...] = own_v[...] + ADAPTER_SCALE * low_up
-    for s in order:
-        part = pl.ds(s * CHUNK, CHUNK)
-        v_hop(n_seq - 2, s).wait_recv()
-        value = (sum_v[n_seq - 1, part, :].astype(f32) + own_v[part, :]).astype(bf16)
-        rows_v[pl.ds(s * per_chunk, per_chunk)] = value.reshape(per_chunk, img_rows, LANES)
-
-    last = n_seq // 2 - 1
-    part_rows = keys // PARTS
-    slots = n_dp // PARTS
+    own[0] = own_part(1, z) + ADAPTER_SCALE * low_up
+    for b in range(PARTS):
+        value = last_sums(1, b).astype(bf16)
+        rows_v[pl.ds(b * per_part, per_part)] = value.reshape(per_part, img_rows, LANES)
+
+    last = mid - 1
 
     def gather(held, n):
         def ahead(t, b):
@@ -364,8 +362,8 @@
             return remote(
                 held.at[source, part],
                 held.at[into, part],
-                ring_ss.at[n, t, b],
-                ring_rs.at[n, t, b],
+                sent_sem.at[7 + n // 2],
+                ring_sem.at[n, t, b],
                 right,
             )
 
@@ -374,8 +372,8 @@
             return remote(
                 held.at[t, part],
                 held.at[t + 1, part],
-                ring_ss.at[n + 1, t, b],
-                ring_rs.at[n + 1, t, b],
+                sent_sem.at[7 + n // 2],
+                ring_sem.at[n + 1, t, b],
                 left,
             )
 
@@ -383,9 +381,9 @@
 
     k_ways, v_ways = gather(k_all, 0), gather(v_all, 2)
 
-    def gather_start(ways, arrived):
+    def gather_start(ways, n, held):
         for b in range(PARTS):
-            loop(max(1, b * slots), (b + 1) * slots, lambda k: arrived(k).wait_recv())
+            routed(n, held.at[0], b)
             for way, whole in ways:
                 if last > 0 or whole(b):
                     way(0, b).start()
@@ -415,14 +413,7 @@
         def _():
             loop(q * per, (q + 1) * per, lambda b: forward(ways, step + 1, b))
 
-    def gather_sent(ways):
-        for t in range(last + 1):
-            for b in range(PARTS):
-                for way, whole in ways:
-                    if t < last or whole(b):
-                        way(t, b).wait_send()
-
-    gather_start(k_ways, k_route)
+    gather_start(k_ways, 0, k_all)
 
     def send_v(k):
         v_out[k] = rows_v[pick[lax.rem(p + k, n_dp)]]
@@ -444,8 +435,9 @@
         bias[n * tokens : (n + 1) * tokens, :] = penalty
     small[...] = jnp.zeros_like(small)
     gate = jnp.tanh(jnp.full((1, LANES), gate_s[0], f32))
-    loop(1, n_seq, lambda k: up_copy(k, lax.rem(z + n_seq - k, n_seq)).wait_recv())
-    loop(1, n_dp, lambda k: ext_route(k).wait_recv())
+    all_here(up_all.at[others], all_sem.at[2])
+    for b in range(PARTS):
+        routed(2, ext, b)
     ext_t[...] = ext[...].T
     load_query.wait()
     load_grad.wait()
@@ -493,14 +485,16 @@
         @pl.when(j == blocks - 1)
         def _():
             whole = value_grad[...].astype(bf16)
-            small[:rank, :] += jnp.dot(up_all[head], whole, preferred_element_type=f32)
+            small[:rank, :] += jnp.dot(
+                up_all[lax.rem(n_seq - slot, n_seq)], whole, preferred_element_type=f32
+            )
             small[rank:, lanes_of(head)] = lax.dot_general(
                 ext_t[:rank, :], whole, NT, preferred_element_type=f32
             )
 
         @pl.when(m == max(blocks * (2 * last - 1), blocks) - 1)
         def _():
-            gather_start(v_ways, v_route)
+            gather_start(v_ways, 1, v_all)
 
         after_block(k_ways, m)
 
@@ -509,7 +503,7 @@
     def col_copy(k):
         target = lax.rem(z + k, n_seq)
         return remote(
-            small.at[:, lanes_of(target)], col_in.at[k], col_ss.at[k], col_rs.at[k], (p, target)
+            small.at[:, lanes_of(target)], col_in.at[k], sent_sem.at[9], all_sem.at[3], (p, target)
         )
 
     wide = total.shape[1]
@@ -518,7 +512,8 @@
     def back_copy(n):
         j, s = lax.rem(n, fit), n // fit
         o = lax.rem(p + n_dp - fit * z - j, n_dp)
-        return remote(back_out.at[j], back_in.at[p], back_ss.at[n], back_rs.at[p], (o, s))
+        into = back_in.at[fit * z + j]
+        return remote(back_out.at[j], into, sent_sem.at[10], all_sem.at[4], (o, s))
 
     def unless_own(n, act):
         pl.when((n != 0) | (z != 0))(act)
@@ -531,46 +526,46 @@
 
     def sum_copy(j):
         k = lax.rem(j - p + n_dp, n_dp)
-        return remote(piece_of(j), sum_in.at[k], sum_ss.at[j], sum_rs.at[k], (j, z))
+        return remote(piece_of(j), sum_in.at[k], sent_sem.at[11], all_sem.at[0], (j, z))
 
     def done_copy(k, j):
         g = lax.rem(p + k, n_dp)
-        return remote(done.at[j], done.at[j], done_ss.at[k], done_rs.at[j], (g, z))
+        return remote(done.at[j], done.at[j], sent_sem.at[12], done_sem.at[j], (g, z))
 
     def adapter_back():
-        own = small[:, lanes_of(z)]
+        mine = small[:, lanes_of(z)]
+        all_here(col_in.at[others], all_sem.at[3])
         for k in range(1, n_seq):
-            col_copy(k).wait_recv()
-            own = own + col_in[k]
-        own = ADAPTER_SCALE * own
+            mine = mine + col_in[k]
+        mine = ADAPTER_SCALE * mine
         for j in range(fit):
-            moved = own[:rank]
+            moved = mine[:rank]
             if j > 0:
                 moved = pltpu.roll(moved, LANES - j * img_rows, 1)
             back_out[j] = moved.astype(bf16)
         total[:, width:] = jnp.zeros((rank, wide - width), f32)
-        total[:, wide - LANES :] = own[rank:]
+        total[:, wide - LANES :] = mine[rank:]
         loop(0, fit * n_seq, lambda n: unless_own(n, lambda: back_copy(n).start()))
 
         @pl.when(z == 0)
         def _():
-            back_in[p] = back_out[0]
+            back_in[0] = back_out[0]
 
     def adapter_sum():
-        def back_wait(k):
-            g = lax.rem(p + k, n_dp)
-            copy = remote(
-                back_out.at[0], back_in.at[g], back_ss.at[0], back_rs.at[g], (g, k // fit)
-            )
-            unless_own(k, lambda: copy.wait_recv())
-
-        loop(0, n_dp, back_wait)
+        @pl.when(z == 0)
+        def _():
+            all_here(back_in.at[pl.ds(1, n_dp - 1)], all_sem.at[4])
+
+        @pl.when(z != 0)
+        def _():
+            all_here(back_in, all_sem.at[4])
+
         lane_rank = lax.broadcasted_iota(jnp.int32, (rank, LANES), 1)
         pieces_in = []
         for first in range(0, img_dev, fit):
             piece = jnp.zeros((rank, LANES), f32)
             for i in range(fit):
-                held = back_in[reader[first + i]].astype(f32)
+                held = back_in[lax.rem(reader[first + i] - p + n_dp, n_dp)].astype(f32)
                 if i > 0:
                     held = pltpu.roll(held, i * img_rows, 1)
                 piece = jnp.where(lane_rank // img_rows == i, held, piece)
@@ -583,21 +578,16 @@
     def adapter_done():
         @pl.when(p < pieces)
         def _():
-            def take(k, acc):
-                remote(
-                    piece_of(p), sum_in.at[k], sum_ss.at[0], sum_rs.at[k], (p, z)
-                ).wait_recv()
-                return acc + sum_in[k]
-
-            done[p] = lax.fori_loop(1, n_dp, take, piece_of(p)[...])
+            all_here(sum_in.at[pl.ds(1, n_dp - 1)], all_sem.at[0])
+            done[p] = piece_of(p)[...] + jnp.sum(sum_in[1:], axis=0)
             loop(1, n_dp, lambda k: done_copy(k, p).start())
 
     loop(1, n_seq, lambda k: col_copy(k).start())
 
-    def store(n, i, head):
+    def store(n, head):
         cols = lanes_of(head, head_width)
         source, into = ((gated, gated_hbm), (query_grad, query_grad_hbm))[n]
-        return pltpu.make_async_copy(source.at[:, cols], into.at[:, cols], store_sem.at[n, i])
+        return pltpu.make_async_copy(source.at[:, cols], into.at[:, cols], store_sem.at[n])
 
     end_block = n_seq * blocks - 1
 
@@ -616,8 +606,8 @@
 
         @pl.when(j == blocks - 1)
         def _():
-            store(0, i, head).start()
-            store(1, i, head).start()
+            store(0, head).start()
+            store(1, head).start()
 
         after_block(v_ways, m)
         pl.when(m == blocks - 1)(adapter_back)
@@ -634,36 +624,40 @@
             down_stage[r : r + 8, c : c + fill] = done[j][:, :fill]
     up_stage[:8, :] = done[pieces - 2]
     up_stage[8:, :] = done[pieces - 1]
-    store_down = pltpu.make_async_copy(down_stage, down_hbm, out_sem.at[0])
-    store_up = pltpu.make_async_copy(up_stage, up_out_hbm, out_sem.at[1])
+    store_down = pltpu.make_async_copy(down_stage, down_hbm, store_sem.at[2])
+    store_up = pltpu.make_async_copy(up_stage, up_out_hbm, store_sem.at[3])
     store_down.start()
     store_up.start()
 
-    def ring_sent(t):
-        for s in range(chunks):
-            k_hop(t, s).wait_send()
-            v_hop(t, s).wait_send()
-
-    loop(0, n_seq - 1, ring_sent)
-    loop(1, n_seq, lambda k: up_copy(k, z).wait_send())
-    for routed in (k_route, v_route, ext_route):
-        loop(1, n_dp, lambda k: routed(k).wait_send())
-    gather_sent(k_ways)
-    gather_sent(v_ways)
-    loop(1, n_seq, lambda k: col_copy(k).wait_send())
-    loop(0, fit * n_seq, lambda n: unless_own(n, lambda: back_copy(n).wait_send()))
-    loop(0, pieces, lambda j: pl.when(j != p)(lambda: sum_copy(j).wait_send()))
+    most = pl.ds(0, n_seq - 1)
+    all_sent(0, sum_k.at[most])
+    all_sent(1, sum_v.at[most])
+    all_sent(3, up_all.at[others])
+    for n, out in enumerate((k_out, v_out, ext_out)):
+        all_sent(4 + n, out.at[pl.ds(1, n_dp - 1)])
+    all_sent(7, k_all.at[most])
+    all_sent(8, v_all.at[most])
+    all_sent(9, col_in.at[others])
+
+    @pl.when(z == 0)
+    def _():
+        all_sent(10, back_in.at[pl.ds(1, n_dp - 1)])
+
+    @pl.when(z != 0)
+    def _():
+        all_sent(10, back_in)
 
     @pl.when(p < pieces)
     def _():
-        loop(1, n_dp, lambda k: done_copy(k, p).wait_send())
-
-    def stored(m):
-        i, j, slot, head, cols = where_is(m * blocks)
-        store(0, i, head).wait()
-        store(1, i, head).wait()
-
-    loop(0, n_seq, stored)
+        all_sent(11, sum_in.at[pl.ds(0, pieces - 1)])
+        all_sent(12, sum_in.at[pl.ds(1, n_dp - 1)])
+
+    @pl.when(p >= pieces)
+    def _():
+        all_sent(11, sum_in.at[pl.ds(0, pieces)])
+
+    pltpu.make_async_copy(gated, gated_hbm, store_sem.at[0]).wait()
+    pltpu.make_async_copy(query_grad, query_grad_hbm, store_sem.at[1]).wait()
     store_down.wait()
     store_up.wait()
 
@@ -693,8 +687,6 @@
     wide = -(-width // LANES) * LANES + LANES
     pieces = 2 * (wide // LANES)
     fit = LANES // img_rows
-    fan = fit * n_seq
-    chunks = rows // CHUNK
     any_space = pl.BlockSpec(memory_space=pl.ANY)
     f32, bf16 = jnp.float32, jnp.bfloat16
 
@@ -727,10 +719,9 @@
             pltpu.SMEM((1, docs), jnp.int32),
             pltpu.SMEM((img_dev,), jnp.int32),
             pltpu.SMEM((img_dev,), jnp.int32),
-            held(rows, LANES, kind=f32),
-            held(rows, LANES, kind=f32),
-            held(n_seq, rows, LANES, kind=f32),
-            held(n_seq, rows, LANES),
+            held(2, rows, LANES, kind=f32),
+            held(n_seq + 2, rows, LANES, kind=f32),
+            held(n_seq + 2, rows, LANES),
             held(rank, rows, kind=f32),
             held(rank, rows),
             held(n_seq, rank, rows),
@@ -760,27 +751,12 @@
             held(rank, width, kind=f32),
             held(rank, LANES, kind=f32),
             dma((12,)),
-            dma((2, n_seq)),
-            dma((2,)),
-            dma((n_seq, chunks)),
-            dma((n_seq, chunks)),
-            dma((n_seq, chunks)),
-            dma((n_seq, chunks)),
-            dma((n_seq,)),
-            dma((n_seq,)),
-            dma((n_seq,)),
-            dma((n_seq,)),
-            dma((3, n_dp)),
-            dma((3, n_dp)),
+            dma((4,)),
+            dma((13,)),
+            dma((5,)),
+            dma((2, 2, n_seq // 2, PARTS)),
+            dma((3, PARTS)),
             dma((4, n_seq // 2, PARTS)),
-            dma((4, n_seq // 2, PARTS)),
-            dma((n_seq,)),
-            dma((n_seq,)),
-            dma((fan,)),
-            dma((n_dp,)),
-            dma((pieces,)),
-            dma((n_dp,)),
-            dma((n_dp,)),
             dma((pieces,)),
         ],
         compiler_params=pltpu.CompilerParams(

time: 128 us -> 119 us (0.930)
  Pallas kernels: 121 us -> 112 us
    pallas_call x1, Pallas kernels: 121 us -> 112 us  [per_device(): pl.pallas_call(functools.partial(fused_kernel, n_dp, n_seq, docs), out_sh...]
where the time goes in v4:
time: 119 us
  Pallas kernels  112 us (94%)
  local copies, waits for them, and re-layouts  5.8 us (5%)
  between operations  1.3 us (1%)
    pallas_call x1, Pallas kernels, per_device(): pl.pallas_call(functools.partial(fused_kernel, n_dp, n_seq, docs), out_sh...  112 us
    unnamed x10, local copies, waits for them, and re-layouts  5.8 us

profile of v4, /device:TPU:1, one launch (start us, length us, event | category | flops | bytes accessed | tf_op | source)
XLA Modules:
  0.0 119.0 jit_solution(17031745745615868803)
XLA Ops:
  1.3 111.9 %shard_map.147 = (bf16[128,8192]{1,0:T(8,128)(2,1)}, bf16[128,8192]{1,0:T(8,128)(2,1)}, f32[16,960]{1,0:T(8,128)}, f32[16,128]{1,0:T(8,128)}) custom-call(bf16[128,8192]{1,0:T(8,128)(2,1)} %query_hbm.1, bf16[128,8192]{1,0:T(8,128)(2,1)} %grad_hbm.1, bf16[512,960]{1,0:T(8,128)(2,1)} %bitcast.4, bf16[960,1024]{1,0:T(8,128)(2,1)} %wk_hbm.1, ...), custom_call_target="tpu_custom_call" | custom-call | tf_op jit(solution)/shard_map/pallas_call | solution.py:697
  113.2 0.0 copy-start
  113.2 3.2 %copy.21 = bf16[128,8192]{1,0:T(8,128)(2,1)} copy(bf16[128,8192]{1,0:T(8,128)(2,1)} %get-tuple-element.16) | data formatting | bytes 4194304
  116.5 0.0 copy-done
  116.5 0.0 copy-start.1
  116.5 0.0 copy-start.2
  116.5 1.3 %copy.22 = bf16[128,8192]{1,0:T(8,128)(2,1)} copy(bf16[128,8192]{1,0:T(8,128)(2,1)S(1)} %copy-done) | data formatting | bytes 4194304
  117.8 0.0 copy-done.1
  117.8 0.6 copy.23
  118.4 0.0 copy-done.2
  118.4 0.6 copy.24
Async XLA Ops:
  113.2 3.3 %copy-start = (bf16[128,8192]{1,0:T(8,128)(2,1)S(1)}, bf16[128,8192]{1,0:T(8,128)(2,1)}, u32[]{:S(2)}) copy-start(bf16[128,8192]{1,0:T(8,128)(2,1)} %get-tuple-element.17) | copy-start | bytes 6291460
  116.5 1.3 %copy-start.1 = (f32[16,960]{1,0:T(8,128)S(1)}, f32[16,960]{1,0:T(8,128)}, u32[]{:S(2)}) copy-start(f32[16,960]{1,0:T(8,128)} %get-tuple-element.10) | copy-start | bytes 184324
  116.5 2.0 %copy-start.2 = (f32[16,128]{1,0:T(8,128)S(1)}, f32[16,128]{1,0:T(8,128)}, u32[]{:S(2)}) copy-start(f32[16,128]{1,0:T(8,128)} %get-tuple-element.19) | copy-start | bytes 24580

commit v5 on v4

--- a/solution.py
+++ b/solution.py
@@ -13,6 +13,7 @@
 LANES = 128
 PARTS = 4
 HEADS_AT_ONCE = 4
+EVENTS = (2, 6, 10)
 LOG2_E = 1.4426950408889634
 MESH = pl.DeviceIdType.MESH
 NT = (((1,), (1,)), ((), ()))
@@ -42,10 +43,20 @@
     pl.semaphore_signal(barrier, inc=1, device_id=target, device_id_type=MESH)
 
 
+def stages_of(n_dp):
+    stages, stride = [], 1
+    while stride < n_dp:
+        size = min(8, n_dp // stride)
+        stages.append((stride, size))
+        stride *= size
+    return stages
+
+
 def fused_kernel(
     n_dp,
     n_seq,
     docs,
+    stages,
     query_hbm,
     grad_hbm,
     tiles_hbm,
@@ -103,8 +114,8 @@
     back_out,
     back_in,
     total,
-    sum_in,
-    done,
+    stage_out,
+    stage_in,
     down_stage,
     up_stage,
     load_sem,
@@ -114,7 +125,7 @@
     sum_sem,
     route_sem,
     ring_sem,
-    done_sem,
+    stage_sem,
 ):
     p = lax.axis_index("dp")
     z = lax.axis_index("seq")
@@ -321,13 +332,16 @@
         if t == mid - 1:
             low_finish()
             loop(1, n_dp, send_ext)
+            load_wv.wait()
+            first_sums(1)
+            first_sends(1)
         sum_step(0, t)
     if mid == 1:
         low_finish()
         loop(1, n_dp, send_ext)
-    load_wv.wait()
-    first_sums(1)
-    first_sends(1)
+        load_wv.wait()
+        first_sums(1)
+        first_sends(1)
 
     per_part = sum_rows // img_rows
     own[0] = own_part(0, z)
@@ -344,83 +358,6 @@
     loop(1, n_dp, send_k)
     k_all[0, :img_rows, :] = rows_k[pick[p]]
     ext[:img_rows, :] = ext_block(p)
-
-    for t in range(1, mid):
-        sum_step(1, t)
-    low_up = lax.dot_general(low_out[...], up[...], TN, preferred_element_type=f32)
-    own[0] = own_part(1, z) + ADAPTER_SCALE * low_up
-    for b in range(PARTS):
-        value = last_sums(1, b).astype(bf16)
-        rows_v[pl.ds(b * per_part, per_part)] = value.reshape(per_part, img_rows, LANES)
-
-    last = mid - 1
-
-    def gather(held, n):
-        def ahead(t, b):
-            part = pl.ds(pl.multiple_of(b * part_rows, part_rows), part_rows)
-            source, into = lax.rem(n_seq - t, n_seq), n_seq - 1 - t
-            return remote(
-                held.at[source, part],
-                held.at[into, part],
-                sent_sem.at[7 + n // 2],
-                ring_sem.at[n, t, b],
-                right,
-            )
-
-        def back(t, b):
-            part = pl.ds(pl.multiple_of(b * part_rows, part_rows), part_rows)
-            return remote(
-                held.at[t, part],
-                held.at[t + 1, part],
-                sent_sem.at[7 + n // 2],
-                ring_sem.at[n + 1, t, b],
-                left,
-            )
-
-        return ((ahead, lambda b: b < PARTS // 2), (back, lambda b: b >= PARTS // 2))
-
-    k_ways, v_ways = gather(k_all, 0), gather(v_all, 2)
-
-    def gather_start(ways, n, held):
-        for b in range(PARTS):
-            routed(n, held.at[0], b)
-            for way, whole in ways:
-                if last > 0 or whole(b):
-                    way(0, b).start()
-
-    def forward(ways, t, b):
-        for way, whole in ways:
-
-            @pl.when((t <= last) | whole(b))
-            def _():
-                way(t - 1, b).wait_recv()
-
-            @pl.when((t < last) | ((t == last) & whole(b)))
-            def _():
-                way(t, b).start()
-
-    def after_block(ways, m):
-        i = m // blocks
-        step = (i + 1) // 2
-        q = m - blocks * (2 * step - 1)
-        per = PARTS // (2 * blocks)
-
-        @pl.when(m == blocks - 1)
-        def _():
-            loop(0, PARTS, lambda b: forward(ways, 1, b))
-
-        @pl.when((i >= 1) & (i < n_seq - 1))
-        def _():
-            loop(q * per, (q + 1) * per, lambda b: forward(ways, step + 1, b))
-
-    gather_start(k_ways, 0, k_all)
-
-    def send_v(k):
-        v_out[k] = rows_v[pick[lax.rem(p + k, n_dp)]]
-        v_route(k).start()
-
-    loop(1, n_dp, send_v)
-    v_all[0, :img_rows, :] = rows_v[pick[p]]
 
     lane_tok = lax.broadcasted_iota(jnp.int32, (tokens, LANES), 1)
     place = lax.broadcasted_iota(jnp.int32, (tokens, LANES), 0) + z * tokens
@@ -442,6 +379,85 @@
     load_query.wait()
     load_grad.wait()
 
+    for t in range(1, mid):
+        sum_step(1, t)
+    last = mid - 1
+
+    def gather(held, n):
+        def ahead(t, b):
+            part = pl.ds(pl.multiple_of(b * part_rows, part_rows), part_rows)
+            source, into = lax.rem(n_seq - t, n_seq), n_seq - 1 - t
+            return remote(
+                held.at[source, part],
+                held.at[into, part],
+                sent_sem.at[7 + n // 2],
+                ring_sem.at[n, t, b],
+                right,
+            )
+
+        def back(t, b):
+            part = pl.ds(pl.multiple_of(b * part_rows, part_rows), part_rows)
+            return remote(
+                held.at[t, part],
+                held.at[t + 1, part],
+                sent_sem.at[7 + n // 2],
+                ring_sem.at[n + 1, t, b],
+                left,
+            )
+
+        return ((ahead, lambda b: b < PARTS // 2), (back, lambda b: b >= PARTS // 2))
+
+    k_ways, v_ways = gather(k_all, 0), gather(v_all, 2)
+
+    def gather_start(ways, n, held):
+        for b in range(PARTS):
+            routed(n, held.at[0], b)
+            for way, whole in ways:
+                if last > 0 or whole(b):
+                    way(0, b).start()
+
+    def forward(ways, t, b):
+        for way, whole in ways:
+
+            @pl.when((t <= last) | whole(b))
+            def _():
+                way(t - 1, b).wait_recv()
+
+            @pl.when((t < last) | ((t == last) & whole(b)))
+            def _():
+                way(t, b).start()
+
+    def after_block(ways, m, first_head):
+        i = m // blocks
+        step = (i + 1) // 2
+        q = m - blocks * (2 * step - 1)
+        per = PARTS // (2 * blocks)
+
+        pl.when(m == blocks - 1)(first_head)
+
+        @pl.when((i >= 1) & (i < n_seq - 1))
+        def _():
+            loop(q * per, (q + 1) * per, lambda b: forward(ways, step + 1, b))
+
+
+    def send_v(k):
+        v_out[k] = rows_v[pick[lax.rem(p + k, n_dp)]]
+        v_route(k).start()
+
+    def values_out():
+        low_up = lax.dot_general(low_out[...], up[...], TN, preferred_element_type=f32)
+        own[0] = own_part(1, z) + ADAPTER_SCALE * low_up
+        for b in range(PARTS):
+            value = last_sums(1, b).astype(bf16)
+            rows_v[pl.ds(b * per_part, per_part)] = value.reshape(per_part, img_rows, LANES)
+        v_all[0, :img_rows, :] = rows_v[pick[p]]
+        for b in range(PARTS):
+            forward(k_ways, 1, b)
+            loop(max(1, b * slots), (b + 1) * slots, send_v)
+
+    def values_on():
+        loop(0, PARTS, lambda b: forward(v_ways, 1, b))
+
     def stack(ref, cols):
         part = ref[:, cols]
         return jnp.concatenate(
@@ -492,12 +508,13 @@
                 ext_t[:rank, :], whole, NT, preferred_element_type=f32
             )
 
+        after_block(k_ways, m, values_out)
+
         @pl.when(m == max(blocks * (2 * last - 1), blocks) - 1)
         def _():
             gather_start(v_ways, 1, v_all)
 
-        after_block(k_ways, m)
-
+    gather_start(k_ways, 0, k_all)
     loop(0, n_seq * blocks, first_half)
 
     def col_copy(k):
@@ -507,7 +524,6 @@
         )
 
     wide = total.shape[1]
-    pieces = 2 * (wide // LANES)
 
     def back_copy(n):
         j, s = lax.rem(n, fit), n // fit
@@ -515,22 +531,36 @@
         into = back_in.at[fit * z + j]
         return remote(back_out.at[j], into, sent_sem.at[10], all_sem.at[4], (o, s))
 
-    def unless_own(n, act):
-        pl.when((n != 0) | (z != 0))(act)
-
-    def piece_of(j):
-        return total.at[
-            pl.ds(pl.multiple_of(lax.rem(j, 2) * 8, 8), 8),
-            lanes_of(j // 2),
-        ]
-
-    def sum_copy(j):
-        k = lax.rem(j - p + n_dp, n_dp)
-        return remote(piece_of(j), sum_in.at[k], sent_sem.at[11], all_sem.at[0], (j, z))
-
-    def done_copy(k, j):
-        g = lax.rem(p + k, n_dp)
-        return remote(done.at[j], done.at[j], sent_sem.at[12], done_sem.at[j], (g, z))
+    def stage_copy(r, k, send):
+        stride, size = stages[r]
+        digit = lax.rem(p // stride, size)
+        peer = lax.rem(digit + k, size)
+        slot = digit if send else lax.rem(digit + size - k, size)
+        return remote(
+            stage_out[r],
+            stage_in[r].at[slot],
+            sent_sem.at[12 + r],
+            stage_sem.at[r, k],
+            (p + (peer - digit) * stride, z),
+        )
+
+    def stage_start(r):
+        stride, size = stages[r]
+        stage_out[r][...] = total[...].astype(bf16)
+        stage_in[r][lax.rem(p // stride, size)] = stage_out[r][...]
+        for k in range(1, size):
+            stage_copy(r, k, True).start()
+
+    def stage_finish(r):
+        size = stages[r][1]
+        for k in range(1, size):
+            stage_copy(r, k, False).wait_recv()
+        here = stage_in[r][0].astype(f32)
+        for d in range(1, size):
+            here = here + stage_in[r][d].astype(f32)
+        total[...] = here
+        if r + 1 < len(stages):
+            stage_start(r + 1)
 
     def adapter_back():
         mine = small[:, lanes_of(z)]
@@ -545,11 +575,15 @@
             back_out[j] = moved.astype(bf16)
         total[:, width:] = jnp.zeros((rank, wide - width), f32)
         total[:, wide - LANES :] = mine[rank:]
-        loop(0, fit * n_seq, lambda n: unless_own(n, lambda: back_copy(n).start()))
+        loop(1, fit * n_seq, lambda n: back_copy(n).start())
 
         @pl.when(z == 0)
         def _():
             back_in[0] = back_out[0]
+
+        @pl.when(z != 0)
+        def _():
+            back_copy(0).start()
 
     def adapter_sum():
         @pl.when(z == 0)
@@ -565,7 +599,8 @@
         for first in range(0, img_dev, fit):
             piece = jnp.zeros((rank, LANES), f32)
             for i in range(fit):
-                held = back_in[lax.rem(reader[first + i] - p + n_dp, n_dp)].astype(f32)
+                slot = lax.rem(reader[first + i] - p + n_dp, n_dp)
+                held = back_in[slot].astype(f32)
                 if i > 0:
                     held = pltpu.roll(held, i * img_rows, 1)
                 piece = jnp.where(lane_rank // img_rows == i, held, piece)
@@ -573,14 +608,7 @@
         total[:, :width] = jnp.dot(
             jnp.concatenate(pieces_in, axis=1), tiles[...], preferred_element_type=f32
         )
-        loop(0, pieces, lambda j: pl.when(j != p)(lambda: sum_copy(j).start()))
-
-    def adapter_done():
-        @pl.when(p < pieces)
-        def _():
-            all_here(sum_in.at[pl.ds(1, n_dp - 1)], all_sem.at[0])
-            done[p] = piece_of(p)[...] + jnp.sum(sum_in[1:], axis=0)
-            loop(1, n_dp, lambda k: done_copy(k, p).start())
+        stage_start(0)
 
     loop(1, n_seq, lambda k: col_copy(k).start())
 
@@ -609,21 +637,17 @@
             store(0, head).start()
             store(1, head).start()
 
-        after_block(v_ways, m)
-        pl.when(m == blocks - 1)(adapter_back)
-        pl.when(m == min(3 * blocks - 1, end_block))(adapter_sum)
-        pl.when(m == min(5 * blocks - 1, end_block))(adapter_done)
+        after_block(v_ways, m, values_on)
+        events = [adapter_back, adapter_sum]
+        events += [functools.partial(stage_finish, r) for r in range(len(stages) - 1)]
+        for at, event in zip(EVENTS, events):
+            pl.when(m == min(at, end_block))(event)
 
     loop(0, n_seq * blocks, second_half)
 
-    loop(0, pieces, lambda j: pl.when(j != p)(lambda: done_copy(0, j).wait_recv()))
-    for j in range(pieces - 2):
-        r, c = 8 * (j % 2), LANES * (j // 2)
-        fill = min(LANES, width - c)
-        if fill > 0:
-            down_stage[r : r + 8, c : c + fill] = done[j][:, :fill]
-    up_stage[:8, :] = done[pieces - 2]
-    up_stage[8:, :] = done[pieces - 1]
+    stage_finish(len(stages) - 1)
+    down_stage[...] = total[:, :width]
+    up_stage[...] = total[:, wide - LANES :]
     store_down = pltpu.make_async_copy(down_stage, down_hbm, store_sem.at[2])
     store_up = pltpu.make_async_copy(up_stage, up_out_hbm, store_sem.at[3])
     store_down.start()
@@ -647,15 +671,8 @@
     def _():
         all_sent(10, back_in)
 
-    @pl.when(p < pieces)
-    def _():
-        all_sent(11, sum_in.at[pl.ds(0, pieces - 1)])
-        all_sent(12, sum_in.at[pl.ds(1, n_dp - 1)])
-
-    @pl.when(p >= pieces)
-    def _():
-        all_sent(11, sum_in.at[pl.ds(0, pieces)])
-
+    for r, (stride, size) in enumerate(stages):
+        all_sent(12 + r, stage_in[r].at[pl.ds(0, size - 1)])
     pltpu.make_async_copy(gated, gated_hbm, store_sem.at[0]).wait()
     pltpu.make_async_copy(query_grad, query_grad_hbm, store_sem.at[1]).wait()
     store_down.wait()
@@ -685,7 +702,7 @@
     keys = n_dp * img_rows
     block = min(HEADS_AT_ONCE * LANES, columns // n_seq) // LANES * tokens
     wide = -(-width // LANES) * LANES + LANES
-    pieces = 2 * (wide // LANES)
+    stages = stages_of(n_dp)
     fit = LANES // img_rows
     any_space = pl.BlockSpec(memory_space=pl.ANY)
     f32, bf16 = jnp.float32, jnp.bfloat16
@@ -695,7 +712,7 @@
 
     dma = pltpu.SemaphoreType.DMA
     gated, query_grad, down_rows, up_grad = pl.pallas_call(
-        functools.partial(fused_kernel, n_dp, n_seq, docs),
+        functools.partial(fused_kernel, n_dp, n_seq, docs, stages),
         out_shape=(
             jax.ShapeDtypeStruct((tokens, columns), bf16),
             jax.ShapeDtypeStruct((tokens, columns), bf16),
@@ -746,18 +763,18 @@
             held(fit, rank, LANES),
             held(n_dp, rank, LANES),
             held(rank, wide, kind=f32),
-            held(n_dp, 8, LANES, kind=f32),
-            held(pieces, 8, LANES, kind=f32),
+            [held(rank, wide) for stage in stages],
+            [held(size, rank, wide) for stride, size in stages],
             held(rank, width, kind=f32),
             held(rank, LANES, kind=f32),
             dma((12,)),
             dma((4,)),
-            dma((13,)),
-            dma((5,)),
+            dma((15,)),
+            dma((6,)),
             dma((2, 2, n_seq // 2, PARTS)),
             dma((3, PARTS)),
             dma((4, n_seq // 2, PARTS)),
-            dma((pieces,)),
+            dma((len(stages), 8)),
         ],
         compiler_params=pltpu.CompilerParams(
             collective_id=0, has_side_effects=True, vmem_limit_bytes=58 << 20

time: 119 us -> 119 us (level)
  no operation moved by 1% of the time
where the time goes in v5:
time: 119 us
  Pallas kernels  112 us (94%)
  local copies, waits for them, and re-layouts  5.8 us (5%)
  between operations  1.3 us (1%)
    pallas_call x1, Pallas kernels, per_device(): pl.pallas_call(functools.partial(fused_kernel, n_dp, n_seq, docs, stages)...  112 us
    unnamed x10, local copies, waits for them, and re-layouts  5.8 us

profile of v5, /device:TPU:1, one launch (start us, length us, event | category | flops | bytes accessed | tf_op | source)
XLA Modules:
  0.0 118.9 jit_solution(9951319243753024054)
XLA Ops:
  1.3 111.8 %shard_map.147 = (bf16[128,8192]{1,0:T(8,128)(2,1)}, bf16[128,8192]{1,0:T(8,128)(2,1)}, f32[16,960]{1,0:T(8,128)}, f32[16,128]{1,0:T(8,128)}) custom-call(bf16[128,8192]{1,0:T(8,128)(2,1)} %query_hbm.1, bf16[128,8192]{1,0:T(8,128)(2,1)} %grad_hbm.1, bf16[512,960]{1,0:T(8,128)(2,1)} %bitcast.4, bf16[960,1024]{1,0:T(8,128)(2,1)} %wk_hbm.1, ...), custom_call_target="tpu_custom_call" | custom-call | tf_op jit(solution)/shard_map/pallas_call | solution.py:714
  113.1 0.0 copy-start
  113.1 3.2 %copy.21 = bf16[128,8192]{1,0:T(8,128)(2,1)} copy(bf16[128,8192]{1,0:T(8,128)(2,1)} %get-tuple-element.16) | data formatting | bytes 4194304
  116.3 0.0 copy-done
  116.3 0.0 copy-start.1
  116.3 0.0 copy-start.2
  116.3 1.3 %copy.22 = bf16[128,8192]{1,0:T(8,128)(2,1)} copy(bf16[128,8192]{1,0:T(8,128)(2,1)S(1)} %copy-done) | data formatting | bytes 4194304
  117.7 0.0 copy-done.1
  117.7 0.6 copy.23
  118.3 0.0 copy-done.2
  118.3 0.6 copy.24
Async XLA Ops:
  113.1 3.3 %copy-start = (bf16[128,8192]{1,0:T(8,128)(2,1)S(1)}, bf16[128,8192]{1,0:T(8,128)(2,1)}, u32[]{:S(2)}) copy-start(bf16[128,8192]{1,0:T(8,128)(2,1)} %get-tuple-element.17) | copy-start | bytes 6291460
  116.3 1.3 %copy-start.1 = (f32[16,960]{1,0:T(8,128)S(1)}, f32[16,960]{1,0:T(8,128)}, u32[]{:S(2)}) copy-start(f32[16,960]{1,0:T(8,128)} %get-tuple-element.10) | copy-start | bytes 184324
  116.3 2.0 %copy-start.2 = (f32[16,128]{1,0:T(8,128)S(1)}, f32[16,128]{1,0:T(8,128)}, u32[]{:S(2)}) copy-start(f32[16,128]{1,0:T(8,128)} %get-tuple-element.19) | copy-start | bytes 24580

commit v6 on v5

--- a/solution.py
+++ b/solution.py
@@ -217,7 +217,7 @@
         own[1] = own_part(n, lax.rem(z + mid + t, n_seq))
         for c in range(PARTS):
             for side in (0, 1):
-                b = c if side == 0 else (c + PARTS // 2) % PARTS
+                b = (c + PARTS // 2) % PARTS if side == 0 else c
                 at = side * (mid + 1) + t
                 total_here = own[side, in_part(b), :]
                 if t > 1 or goes(side, b):

time: 119 us -> 119 us (level)
  no operation moved by 1% of the time
where the time goes in v6:
time: 119 us
  Pallas kernels  112 us (94%)
  local copies, waits for them, and re-layouts  5.8 us (5%)
  between operations  1.3 us (1%)
    pallas_call x1, Pallas kernels, per_device(): pl.pallas_call(functools.partial(fused_kernel, n_dp, n_seq, docs, stages)...  112 us
    unnamed x10, local copies, waits for them, and re-layouts  5.8 us

profile of v6, /device:TPU:1, one launch (start us, length us, event | category | flops | bytes accessed | tf_op | source)
XLA Modules:
  0.0 119.0 jit_solution(1911783138788217329)
XLA Ops:
  1.3 111.9 %shard_map.147 = (bf16[128,8192]{1,0:T(8,128)(2,1)}, bf16[128,8192]{1,0:T(8,128)(2,1)}, f32[16,960]{1,0:T(8,128)}, f32[16,128]{1,0:T(8,128)}) custom-call(bf16[128,8192]{1,0:T(8,128)(2,1)} %query_hbm.1, bf16[128,8192]{1,0:T(8,128)(2,1)} %grad_hbm.1, bf16[512,960]{1,0:T(8,128)(2,1)} %bitcast.4, bf16[960,1024]{1,0:T(8,128)(2,1)} %wk_hbm.1, ...), custom_call_target="tpu_custom_call" | custom-call | tf_op jit(solution)/shard_map/pallas_call | solution.py:714
  113.2 0.0 copy-start
  113.2 3.2 %copy.21 = bf16[128,8192]{1,0:T(8,128)(2,1)} copy(bf16[128,8192]{1,0:T(8,128)(2,1)} %get-tuple-element.16) | data formatting | bytes 4194304
  116.5 0.0 copy-done
  116.5 0.0 copy-start.1
  116.5 0.0 copy-start.2
  116.5 1.3 %copy.22 = bf16[128,8192]{1,0:T(8,128)(2,1)} copy(bf16[128,8192]{1,0:T(8,128)(2,1)S(1)} %copy-done) | data formatting | bytes 4194304
  117.8 0.0 copy-done.1
  117.8 0.6 copy.23
  118.4 0.0 copy-done.2
  118.4 0.6 copy.24
Async XLA Ops:
  113.2 3.3 %copy-start = (bf16[128,8192]{1,0:T(8,128)(2,1)S(1)}, bf16[128,8192]{1,0:T(8,128)(2,1)}, u32[]{:S(2)}) copy-start(bf16[128,8192]{1,0:T(8,128)(2,1)} %get-tuple-element.17) | copy-start | bytes 6291460
  116.5 1.3 %copy-start.1 = (f32[16,960]{1,0:T(8,128)S(1)}, f32[16,960]{1,0:T(8,128)}, u32[]{:S(2)}) copy-start(f32[16,960]{1,0:T(8,128)} %get-tuple-element.10) | copy-start | bytes 184324
  116.5 2.0 %copy-start.2 = (f32[16,128]{1,0:T(8,128)S(1)}, f32[16,128]{1,0:T(8,128)}, u32[]{:S(2)}) copy-start(f32[16,128]{1,0:T(8,128)} %get-tuple-element.19) | copy-start | bytes 24580
